TPU v7x, 32 devices: a whole 2x2x4 slice. The times are simulated.
32 devices in a mesh: dp: 8 (over z, y), tp: 4 (over x, core).
Axes of the slice: x: 2, y: 2, z: 4, core: 2. Of those that a mesh axis runs over, the one named last changes fastest.
Arguments:
- tokens: bfloat16 [16, 1024, 768], P('dp', 'tp'), may hold values from -6 to 6
- cotangent: bfloat16 [16, 1024, 768], P('dp', 'tp'), may hold values from -6 to 6
- segment_ids: int32 [16, 1024], P('dp', 'tp'), may hold values from 0 to 2, as said below
- valid_mask: int32 [16, 1024], P('dp', 'tp'), may hold values from 0 to 1, as said below
- row_half: int32 [16], P('dp'), may hold values from 0 to 1, as said below
- norm1_gain: float32 [768], replicated, may hold values from 0.5 to 1.5
- norm1_shift: float32 [768], replicated, may hold values from -1 to 1
- qkv_weight: bfloat16 [768, 3, 768], P(None, None, 'tp'), may hold values from -0.21875 to 0.21875
- qkv_bias: float32 [3, 768], P(None, 'tp'), may hold values from -1 to 1
- out_weight: bfloat16 [768, 768], P('tp'), may hold values from -2.5 to 2.5
- out_bias: float32 [768], replicated, may hold values from -1 to 1
- norm2_gain: float32 [768], replicated, may hold values from 0.5 to 1.5
- norm2_shift: float32 [768], replicated, may hold values from -1 to 1
- fc_weight: bfloat16 [768, 3072], P(None, 'tp'), may hold values from -0.21875 to 0.21875
- fc_bias: float32 [3072], P('tp'), may hold values from -1 to 1
- proj_weight: bfloat16 [3072, 768], P('tp'), may hold values from -0.109375 to 0.109375
- proj_bias: float32 [768], replicated, may hold values from -1 to 1
Outputs:
- output: bfloat16 [16, 1024, 768], P('dp', 'tp')
- tokens_grad: float32 [16, 1024, 768], P('dp', 'tp')
- norm1_gain_grad: float32 [768], replicated
- norm1_shift_grad: float32 [768], replicated
- qkv_weight_grad: float32 [768, 3, 768], P(None, None, 'tp')
- qkv_bias_grad: float32 [3, 768], P(None, 'tp')
- out_weight_grad: float32 [768, 768], P('tp')
- out_bias_grad: float32 [768], replicated
- norm2_gain_grad: float32 [768], replicated
- norm2_shift_grad: float32 [768], replicated
- fc_weight_grad: float32 [768, 3072], P(None, 'tp')
- fc_bias_grad: float32 [3072], P('tp')
- proj_weight_grad: float32 [3072, 768], P('tp')
- proj_bias_grad: float32 [768], replicated
Inputs may be any that keep to these rules, and one draw needn't show every extreme that they name: `segment_ids`: each row holds three documents numbered 0, 1, 2 in order; document 1 starts at position 128 or earlier, and document 2 starts at position 896 or later and before 1024. `valid_mask`: in each row the tokens with 1 form a prefix of 256 tokens or more. `row_half`: rows below a cut are replay rows (0), the others fresh (1); the cut lies between 4 and 12.
All inputs are finite; a program needn't handle non-finite values.
Results may differ from a plain program's by a relative error of at most 0.0095.
Values may be sent and summed in bfloat16 or wider, within the bound.
A program may use at most 128 MiB of HBM per device.

v0:
```python
import jax
import jax.numpy as jnp
from jax import lax
from jax.sharding import PartitionSpec as P

HD = 64


EPSILON = 1e-05


def layer_norm(values, gain, shift):
    average = jnp.mean(values, axis=-1, keepdims=True)
    centered = values - average
    spread = jnp.mean(centered * centered, axis=-1, keepdims=True)
    return centered * lax.rsqrt(spread + EPSILON) * gain + shift


def smooth_gelu(values):
    return (
        0.5
        * values
        * (1.0 + jnp.tanh(0.7978845608028654 * (values + 0.044715 * values * values * values)))
    )


def block_scores(query_rows, key_rows, segment_row, offset):
    rows_here = query_rows.shape[0]
    products = jnp.einsum(
        "qhd,khd->hqk", query_rows, key_rows, preferred_element_type=jnp.float32
    ) * HD ** (-0.5)
    query_at = offset + jnp.arange(rows_here)
    key_at = jnp.arange(key_rows.shape[0])
    query_segment = segment_row[offset : offset + rows_here]
    allowed = (key_at[None, :] <= query_at[:, None]) & (
        query_segment[:, None] == segment_row[None, :]
    )
    return jnp.where(allowed[None], products, -1e30)


def unpack_row(qkv_row):
    length = qkv_row.shape[0]
    head_count = qkv_row.shape[2] // HD
    unpacked = qkv_row.reshape(length, 3, head_count, HD)
    return (unpacked[:, 0], unpacked[:, 1], unpacked[:, 2], length, head_count)


def attend_row(qkv_row, segment_row):
    query_rows, key_rows, value_rows, length, head_count = unpack_row(qkv_row)
    stride_rows = min(512, length)
    outputs, maxima_parts, total_parts = ([], [], [])
    for offset in range(0, length, stride_rows):
        scores = block_scores(
            query_rows[offset : offset + stride_rows], key_rows, segment_row, offset
        )
        maxima = jnp.max(scores, axis=-1, keepdims=True)
        exponent = jnp.exp(scores - maxima)
        totals = jnp.sum(exponent, axis=-1, keepdims=True)
        weights_low = (exponent / totals).astype(jnp.bfloat16)
        mixed_out = jnp.einsum(
            "hqk,khd->qhd", weights_low, value_rows, preferred_element_type=jnp.float32
        )
        outputs.append(mixed_out.reshape(stride_rows, head_count * HD))
        maxima_parts.append(maxima)
        total_parts.append(totals)
    return (
        jnp.concatenate(outputs, 0),
        jnp.concatenate(maxima_parts, 1),
        jnp.concatenate(total_parts, 1),
    )


def attend_row_back(qkv_row, segment_row, grad_row, maxima, totals):
    query_rows, key_rows, value_rows, length, head_count = unpack_row(qkv_row)
    upstream = grad_row.reshape(length, head_count, HD)
    score_scale = HD ** (-0.5)
    stride_rows = min(512, length)
    key_grad = jnp.zeros((length, head_count, HD), jnp.float32)
    value_grad = jnp.zeros((length, head_count, HD), jnp.float32)
    query_parts = []
    for offset in range(0, length, stride_rows):
        query_block = query_rows[offset : offset + stride_rows]
        scores = block_scores(query_block, key_rows, segment_row, offset)
        weights = (
            jnp.exp(scores - maxima[:, offset : offset + stride_rows])
            / totals[:, offset : offset + stride_rows]
        )
        local_grad = upstream[offset : offset + stride_rows]
        weight_grad = jnp.einsum(
            "qhd,khd->hqk", local_grad, value_rows, preferred_element_type=jnp.float32
        )
        row_dot = jnp.sum(weights * weight_grad, axis=-1, keepdims=True)
        score_low = (weights * (weight_grad - row_dot)).astype(jnp.bfloat16)
        query_parts.append(
            jnp.einsum("hqk,khd->qhd", score_low, key_rows, preferred_element_type=jnp.float32)
            * score_scale
        )
        key_grad = (
            key_grad
            + jnp.einsum("hqk,qhd->khd", score_low, query_block, preferred_element_type=jnp.float32)
            * score_scale
        )
        value_grad = value_grad + jnp.einsum(
            "hqk,qhd->khd",
            weights.astype(jnp.bfloat16),
            local_grad,
            preferred_element_type=jnp.float32,
        )
    query_grad = jnp.concatenate(query_parts, 0)
    stacked = jnp.stack([query_grad, key_grad, value_grad], axis=1)
    return stacked.reshape(length, 3, head_count * HD)


def local(
    tokens,
    cotangent,
    segment_ids,
    valid_mask,
    row_half,
    norm1_gain,
    norm1_shift,
    qkv_weight,
    qkv_bias,
    out_weight,
    out_bias,
    norm2_gain,
    norm2_shift,
    fc_weight,
    fc_bias,
    proj_weight,
    proj_bias,
):
    local_rows = tokens.astype(jnp.float32)
    normed, norm1_back = jax.vjp(layer_norm, local_rows, norm1_gain, norm1_shift)
    normed_low = normed.astype(jnp.bfloat16)
    full_normed, full_segments = (
        lax.all_gather(normed_low, "tp", axis=1, tiled=True),
        lax.all_gather(segment_ids, "tp", axis=1, tiled=True),
    )
    length = full_normed.shape[1]
    owned_count = length // lax.axis_size("tp")
    qkv = (
        jnp.einsum("rld,dch->rlch", full_normed, qkv_weight, preferred_element_type=jnp.float32)
        + qkv_bias
    )
    qkv_low = qkv.astype(jnp.bfloat16)
    attended, maxima, totals = lax.map(
        lambda bundle: attend_row(bundle[0], bundle[1]), (qkv_low, full_segments)
    )
    attended_low = attended.astype(jnp.bfloat16)
    part_rows = lax.slice_in_dim(attended_low, 0, owned_count * lax.axis_size("tp"), axis=1)
    attn_owned = jnp.transpose(
        lax.psum_scatter(
            jnp.einsum("rlh,hd->lrd", part_rows, out_weight, preferred_element_type=jnp.float32),
            "tp",
            scatter_dimension=0,
            tiled=True,
        ),
        (1, 0, 2),
    )
    middle = local_rows + attn_owned + out_bias
    normed_two, norm2_back = jax.vjp(layer_norm, middle, norm2_gain, norm2_shift)
    normed_two_low = normed_two.astype(jnp.bfloat16)
    full_normed_two = lax.all_gather(normed_two_low, "tp", axis=1, tiled=True)
    hidden_pre = (
        jnp.einsum("rld,df->rlf", full_normed_two, fc_weight, preferred_element_type=jnp.float32)
        + fc_bias
    )
    hidden_act, gelu_back = jax.vjp(smooth_gelu, hidden_pre)
    hidden_low = hidden_act.astype(jnp.bfloat16)
    part_rows = lax.slice_in_dim(hidden_low, 0, lax.axis_size("tp") * owned_count, axis=1)
    mlp_total = lax.psum_scatter(
        jnp.einsum(
            "rlf,fd->lrd", part_rows, proj_weight, preferred_element_type=jnp.float32
        ).astype(jnp.bfloat16),
        "tp",
        scatter_dimension=0,
        tiled=True,
    ).astype(jnp.float32)
    result = middle + jnp.transpose(mlp_total, (1, 0, 2)) + proj_bias
    output = result.astype(jnp.bfloat16)
    valid_float = valid_mask.astype(jnp.float32)
    row_counts = jnp.sum(valid_float, axis=1)
    replay_local = jnp.sum(jnp.where(row_half == 0, row_counts, 0.0))
    fresh_local = jnp.sum(jnp.where(row_half == 1, row_counts, 0.0))
    replay_count, fresh_count = lax.psum((replay_local, fresh_local), ("dp", "tp"))
    row_scale = (replay_count + fresh_count) / (
        2.0 * jnp.where(row_half == 0, replay_count, fresh_count)
    )
    out_grad = cotangent.astype(jnp.float32) * (valid_float * row_scale[:, None])[..., None]
    branch_low = out_grad.astype(jnp.bfloat16)
    proj_bias_grad = jnp.sum(branch_low, axis=(0, 1), dtype=jnp.float32)
    full_grad = lax.all_gather(branch_low, "tp", axis=1, tiled=True)
    hidden_grad = jnp.einsum(
        "rld,fd->rlf", full_grad, proj_weight, preferred_element_type=jnp.float32
    )
    proj_weight_grad = jnp.einsum(
        "rlf,rld->fd", hidden_low, full_grad, preferred_element_type=jnp.float32
    )
    (pre_grad,) = gelu_back(hidden_grad)
    pre_low = pre_grad.astype(jnp.bfloat16)
    fc_bias_grad = jnp.sum(pre_low, axis=(0, 1), dtype=jnp.float32)
    fc_weight_grad = jnp.einsum(
        "rld,rlf->df", full_normed_two, pre_low, preferred_element_type=jnp.float32
    )
    part_rows = lax.slice_in_dim(pre_low, 0, owned_count * lax.axis_size("tp"), axis=1)
    normed_two_grad = jnp.transpose(
        lax.psum_scatter(
            jnp.einsum("rlf,df->lrd", part_rows, fc_weight, preferred_element_type=jnp.float32),
            "tp",
            scatter_dimension=0,
            tiled=True,
        ),
        (1, 0, 2),
    )
    middle_part, norm2_gain_grad, norm2_shift_grad = norm2_back(normed_two_grad)
    middle_grad = out_grad + middle_part
    attn_low = middle_grad.astype(jnp.bfloat16)
    out_bias_grad = jnp.sum(attn_low, axis=(0, 1), dtype=jnp.float32)
    full_attn_grad = lax.all_gather(attn_low, "tp", axis=1, tiled=True)
    attended_grad = jnp.einsum(
        "rld,hd->rlh", full_attn_grad, out_weight, preferred_element_type=jnp.float32
    )
    out_weight_grad = jnp.einsum(
        "rlh,rld->hd", attended_low, full_attn_grad, preferred_element_type=jnp.float32
    )
    attended_grad_low = attended_grad.astype(jnp.bfloat16)
    qkv_grad = lax.map(
        lambda bundle: attend_row_back(bundle[0], bundle[1], bundle[2], bundle[3], bundle[4]),
        (qkv_low, full_segments, attended_grad_low, maxima, totals),
    )
    qkv_grad_low = qkv_grad.astype(jnp.bfloat16)
    qkv_bias_grad = jnp.sum(qkv_grad_low, axis=(0, 1), dtype=jnp.float32)
    qkv_weight_grad = jnp.einsum(
        "rld,rlch->dch", full_normed, qkv_grad_low, preferred_element_type=jnp.float32
    )
    part_rows = qkv_grad_low
    normed_grad = jnp.transpose(
        lax.psum_scatter(
            jnp.einsum("rlch,dch->lrd", part_rows, qkv_weight, preferred_element_type=jnp.float32),
            "tp",
            scatter_dimension=0,
            tiled=True,
        ),
        (1, 0, 2),
    )
    tokens_part, norm1_gain_grad, norm1_shift_grad = norm1_back(normed_grad)
    tokens_grad = middle_grad + tokens_part
    (
        norm1_gain_grad,
        norm1_shift_grad,
        norm2_gain_grad,
        norm2_shift_grad,
        out_bias_grad,
        proj_bias_grad,
    ) = lax.psum(
        (
            norm1_gain_grad,
            norm1_shift_grad,
            norm2_gain_grad,
            norm2_shift_grad,
            out_bias_grad,
            proj_bias_grad,
        ),
        ("dp", "tp"),
    )
    (
        qkv_weight_grad,
        qkv_bias_grad,
        out_weight_grad,
        fc_weight_grad,
        fc_bias_grad,
        proj_weight_grad,
    ) = lax.psum(
        (
            qkv_weight_grad,
            qkv_bias_grad,
            out_weight_grad,
            fc_weight_grad,
            fc_bias_grad,
            proj_weight_grad,
        ),
        "dp",
    )
    return (
        output,
        tokens_grad,
        norm1_gain_grad,
        norm1_shift_grad,
        qkv_weight_grad,
        qkv_bias_grad,
        out_weight_grad,
        out_bias_grad,
        norm2_gain_grad,
        norm2_shift_grad,
        fc_weight_grad,
        fc_bias_grad,
        proj_weight_grad,
        proj_bias_grad,
    )


def solution(mesh):
    in_specs = (
        P("dp", "tp", None),
        P("dp", "tp", None),
        P("dp", "tp"),
        P("dp", "tp"),
        P("dp"),
        P(),
        P(),
        P(None, None, "tp"),
        P(None, "tp"),
        P("tp", None),
        P(),
        P(),
        P(),
        P(None, "tp"),
        P("tp"),
        P("tp", None),
        P(),
    )
    out_specs = (
        P("dp", "tp", None),
        P("dp", "tp", None),
        P(),
        P(),
        P(None, None, "tp"),
        P(None, "tp"),
        P("tp", None),
        P(),
        P(),
        P(),
        P(None, "tp"),
        P("tp"),
        P("tp", None),
        P(),
    )
    return jax.shard_map(local, mesh=mesh, in_specs=in_specs, out_specs=out_specs, check_vma=False)
```

profile of v0, /device:TPU:0, one launch (start us, length us, event | category | flops | bytes accessed | tf_op | source)
XLA Modules:
  0.0 754.1 jit_solution(2819547433553566693)
XLA Ops:
  11.4 2.4 fusion.51
  13.9 6.1 all_gather.16
  20.0 25.2 %all-gather.5.cloned.1.call-done = bf16[2,1024,768]{2,1,0:T(8,128)(2,1)} async-done(((bf16[2,256,768]{2,1,0:T(8,128)(2,1)}), bf16[2,1024,768]{2,1,0:T(8,128)(2,1)}) %all-gather.5.cloned.1.call-update) | async-done | bytes 3145744 | tf_op jit(solution)/shard_map/all_gather | solution.py:137
  45.1 4.1 add_convert_fusion
  49.3 26.4 %while.24 = (s32[]{:T(128)}, bf16[2,1024,192]{1,2,0:T(8,128)(2,1)}, f32[2,3,1024,1]{2,1,3,0:T(4,128)}, f32[2,3,1024,1]{2,1,3,0:T(4,128)}, bf16[2,1024,3,192]{1,3...) while((s32[]{:T(128)}, bf16[2,1024,192]{1,2,0:T(8,128)(2,1)}, ...), condition=%wide.region_7.8_spmd, body=%wide.region_2.7_spmd.sunk | while | flops 846987776 | bytes 54296880 | solution.py:147
  53.8 2.0 fusion.143
  58.9 2.0 fusion.140
  67.0 2.0 fusion.143
  72.1 2.0 fusion.140
  75.7 4.9 convolution_bitcast_fusion.1
  81.0 58.1 %reduce-scatter.5.cloned.1.call-done = f32[256,2,768]{2,0,1:T(8,128)} async-done(((f32[1024,2,768]{2,0,1:T(8,128)}), f32[256,2,768]{2,0,1:T(8,128)}) %reduce-scatter.5.cloned.1.call-update) | async-done | bytes 1572880 | tf_op jit(solution)/shard_map/reduce_scatter | solution.py:153
  139.1 1.9 fusion.87
  142.7 1.9 add_convert_fusion.1
  146.7 39.8 %all-reduce.1 = (f32[]{:T(128)}, f32[]{:T(128)}) all-reduce(f32[]{:T(128)} %get-tuple-element.94, f32[]{:T(128)} %get-tuple-element.93), channel_id=1, replica_groups=mesh['dp'=8,'tp'=4] {'dp','tp'}, use_global_device_ids=true, to_apply=%region_16.17 | all-reduce | flops 2 | bytes 16 | tf_op jit(solution)/shard_map/psum | solution.py:186
  187.8 2.0 fusion.80
  191.1 2.8 convert_reduce_fusion.3
  194.1 7.5 fusion.66
  201.6 22.0 %all-gather.9.cloned.1.call-done = bf16[2,1024,768]{2,1,0:T(8,128)(2,1)} async-done(((bf16[2,256,768]{2,1,0:T(8,128)(2,1)}), bf16[2,1024,768]{2,1,0:T(8,128)(2,1)}) %all-gather.9.cloned.1.call-update) | async-done | bytes 3145744 | tf_op jit(solution)/shard_map/all_gather | solution.py:193
  223.6 10.8 %convert_reduce_fusion = (f32[768]{0:T(1024)}, bf16[2,1024,768]{2,1,0:T(8,128)(2,1)S(1)}) fusion(bf16[2,1024,768]{2,1,0:T(8,128)(2,1)} %all-gather.9.cloned.1.call-done, bf16[768,768]{1,0:T(8,128)(2,1)S(1)} %copy-done, f32[2,1024,768]{2,1,0:T(8,128)} %fusion.66, f32[768]{0:T(1024)} %param.35), kind=kOutput, calls=%fused_computation.88 | convolution fusion | flops 2458385664 | bytes 13768704 | tf_op jit(solution)/shard_map/rld,fd->rlf/dot_general | solution.py:194
  236.1 4.5 convolution_bitcast_fusion.2
  240.7 8.5 %convert_bitcast_fusion = bf16[1024,2,768]{2,0,1:T(8,128)(2,1)} fusion(bf16[768,768]{1,0:T(8,128)(2,1)S(1)} %copy-done, f32[2,1024,768]{2,1,0:T(8,128)} %fusion.66, f32[768]{0:T(1024)} %param.35), kind=kOutput, calls=%fused_computation.96 | convolution fusion | flops 2433220608 | bytes 10619904 | tf_op jit(solution)/shard_map/rlf,fd->lrd/dot_general | solution.py:173
  249.3 49.8 %reduce-scatter.9.cloned.1.call-done = f32[256,2,768]{2,0,1:T(8,128)} async-done(((f32[1024,2,768]{2,0,1:T(8,128)}), f32[256,2,768]{2,0,1:T(8,128)}) %reduce-scatter.9.cloned.1.call-update) | async-done | bytes 1572880 | tf_op jit(solution)/shard_map/reduce_scatter | solution.py:208
  299.1 3.0 fusion.58
  302.2 37.3 %reduce-scatter.7.cloned.1.call-done = bf16[256,2,768]{2,0,1:T(8,128)(2,1)} async-done(((bf16[1024,2,768]{2,0,1:T(8,128)(2,1)}), bf16[256,2,768]{2,0,1:T(8,128)(2,1)}) %reduce-scatter.7.cloned.1.call-update) | async-done | bytes 786448 | tf_op jit(solution)/shard_map/reduce_scatter | solution.py:172
  339.5 3.6 fusion.86
  344.3 1.8 convert_reduce_fusion.4
  346.2 28.6 %all-gather.11.cloned.1.call-done = bf16[2,1024,768]{2,1,0:T(8,128)(2,1)} async-done(((bf16[2,256,768]{2,1,0:T(8,128)(2,1)}), bf16[2,1024,768]{2,1,0:T(8,128)(2,1)}) %all-gather.11.cloned.1.call-update) | async-done | bytes 3145744 | tf_op jit(solution)/shard_map/all_gather | solution.py:220
  374.8 3.9 convolution_convert_fusion
  378.8 53.6 %while.25 = (s32[]{:T(128)}, bf16[2,1024,3,192]{1,3,2,0:T(8,128)(2,1)}, bf16[2,1024,3,192]{1,3,2,0:T(8,128)(2,1)S(1)}, s32[2,1024]{1,0:T(2,128)S(1)}, f32[2,3,10...) while((s32[]{:T(128)}, ...), condition=%wide.region_23.24_spmd, body=%wide.region_20.23_spmd.sunk | while | flops 2053568000 | bytes 179409408 | solution.py:228
  382.8 1.8 fusion.157
  385.7 2.7 multiply_reduce_fusion.7
  392.6 2.8 multiply_reduce_fusion.6
  395.4 3.9 multiply_convert_fusion.8
  412.3 2.7 multiply_reduce_fusion.7
  419.2 2.8 multiply_reduce_fusion.6
  422.0 3.9 multiply_convert_fusion.8
  432.4 7.2 convolution_bitcast_fusion
  439.6 7.1 convolution_bitcast_fusion.4
  446.7 9.4 %convolution_bitcast_fusion.3 = f32[768,768]{1,0:T(8,128)} fusion(bf16[2,1024,768]{2,1,0:T(8,128)(2,1)S(1)} %copy-done.59, f32[2,1024,768]{2,1,0:T(8,128)} %fusion.66, f32[768]{0:T(1024)S(1)} %copy-done.62), kind=kOutput, calls=%fused_computation.111 | convolution fusion | flops 2431647744 | bytes 11799552 | tf_op jit(solution)/shard_map/rlf,rld->fd/dot_general | solution.py:197
  457.8 3.2 fusion.60
  462.9 2.2 convert_reduce_fusion.1
  465.1 22.3 %all-reduce.2 = (f32[3,192]{1,0:T(4,128)}, f32[768]{0:T(1024)}) all-reduce(f32[3,192]{1,0:T(4,128)S(1)} %convert_reduce_fusion.1, f32[768]{0:T(1024)S(1)} %copy-done.55), channel_id=1, replica_groups=mesh['dp'=8,'tp'=4] {'dp'}, use_global_device_ids=true, to_apply=%region_33.34 | all-reduce | flops 1344 | bytes 10752 | tf_op jit(solution)/shard_map/psum | solution.py:274
  487.5 10.6 %reduce-scatter.11.cloned.1.call-done = f32[256,2,768]{2,0,1:T(8,128)} async-done(((f32[1024,2,768]{2,0,1:T(8,128)}), f32[256,2,768]{2,0,1:T(8,128)}) %reduce-scatter.11.cloned.1.call-update) | async-done | bytes 1572880 | tf_op jit(solution)/shard_map/reduce_scatter | solution.py:239
  499.8 1.8 fusion.54
  502.4 44.3 %all-reduce = (f32[768]{0:T(1024)}, f32[768]{0:T(1024)}, f32[768]{0:T(1024)}, f32[768]{0:T(1024)}, f32[768]{0:T(1024)}, /*index=5*/f32[768]{0:T(1024)}) all-reduce(f32[768]{0:T(1024)S(1)} %get-tuple-element.91, f32[768]{0:T(1024)S(1)} %reduce_sum.251, f32[768]{0:T(1024)S(1)} %copy-done.53, ...), channel_id=1, replica_groups=mesh['dp'=8,'tp'=4] {'dp','tp'}, use_global_device_ids=true, to_apply=%region_28.29 | all-reduce | flops 4608 | bytes 36864 | tf_op jit(solution)/shard_map/psum | solution.py:256
  546.7 2.9 add_add_fusion.2
  549.7 190.8 %all-reduce.6.cloned.1.call-done = (f32[768,3,192]{0,2,1:T(8,128)}, f32[192,768]{1,0:T(8,128)}, f32[768,768]{1,0:T(8,128)}, f32[768,768]{1,0:T(8,128)}) async-done(((f32[768,3,192]{0,2,1:T(8,128)}, f32[192,768]{1,0:T(8,128)}, f32[768,768]{1,0:T(8,128)}, f32[768,768]{1,0:T(8,128)}), (f32[768,3,192]{0,2,1:T(8,128)}, f32[192,768]{1,0:T(8,128)}, f32[768,768]{1,0:T(8,128)}, ...) | async-done | bytes 7077904 | tf_op jit(solution)/shard_map/psum | solution.py:274
  740.5 2.9 copy.65
  (269 shorter events, 73.0 us)
Async XLA Ops:
  7.2 216.4 %copy-start = (bf16[768,768]{1,0:T(8,128)(2,1)S(1)}, bf16[768,768]{1,0:T(8,128)(2,1)}, u32[]{:S(2)}) copy-start(bf16[768,768]{1,0:T(8,128)(2,1)} %param.36) | copy-start | bytes 3538948
  7.2 6.6 copy-start.57
  7.2 37.9 %copy-start.61 = (f32[3,192]{1,0:T(4,128)S(1)}, f32[3,192]{1,0:T(4,128)}, u32[]{:S(2)}) copy-start(f32[3,192]{1,0:T(4,128)} %param.29) | copy-start | bytes 6916
  7.2 37.9 %all-gather.5.cloned.1.call-start = ((), (), s32[]{:S(2)}) async-start(), calls=%async_computation.4 | async-start | bytes 3932160 | tf_op jit(solution)/shard_map/all_gather | solution.py:137
  13.8 125.3 %reduce-scatter.5.cloned.1.call-start = ((), (), s32[]{:S(2)}) async-start(), calls=%async_computation.5 | async-start | bytes 7864320 | tf_op jit(solution)/shard_map/reduce_scatter | solution.py:153
  80.6 58.5 %copy-start.56 = (f32[768]{0:T(1024)S(1)}, f32[768]{0:T(1024)}, u32[]{:S(2)}) copy-start(f32[768]{0:T(1024)} %param.31) | copy-start | bytes 9220
  80.6 62.1 %copy-start.37 = (f32[768]{0:T(1024)S(1)}, f32[768]{0:T(1024)}, u32[]{:S(2)}) copy-start(f32[768]{0:T(1024)} %param.32) | copy-start | bytes 9220
  80.6 113.5 %all-gather.7.cloned.1.call-start = ((), (), s32[]{:S(2)}) async-start(), calls=%async_computation.6 | async-start | bytes 3932160 | tf_op jit(solution)/shard_map/all_gather | solution.py:164
  144.6 78.9 %all-gather.9.cloned.1.call-start = ((), (), s32[]{:S(2)}) async-start(), calls=%async_computation.8 | async-start | bytes 3932160 | tf_op jit(solution)/shard_map/all_gather | solution.py:193
  194.0 105.1 %reduce-scatter.9.cloned.1.call-start = ((), (), s32[]{:S(2)}) async-start(), calls=%async_computation.9 | async-start | bytes 7864320 | tf_op jit(solution)/shard_map/reduce_scatter | solution.py:208
  223.6 12.5 %copy-start.60 = (bf16[768,768]{1,0:T(8,128)(2,1)S(1)}, bf16[768,768]{1,0:T(8,128)(2,1)}, u32[]{:S(2)}) copy-start(bf16[768,768]{1,0:T(8,128)(2,1)} %param.34) | copy-start | bytes 3538948
  240.6 98.9 %reduce-scatter.7.cloned.1.call-start = ((), (), s32[]{:S(2)}) async-start(), calls=%async_computation.7 | async-start | bytes 3932160 | tf_op jit(solution)/shard_map/reduce_scatter | solution.py:172
  249.2 49.9 %copy-start.44 = (f32[2,256]{1,0:T(2,128)S(1)}, f32[2,256]{1,0:T(2,128)}, u32[]{:S(2)}) copy-start(f32[2,256]{1,0:T(2,128)} %copy-done.43) | copy-start | bytes 6148
  249.2 52.9 %copy-start.50 = (f32[2,256]{1,0:T(2,128)S(1)}, f32[2,256]{1,0:T(2,128)}, u32[]{:S(2)}) copy-start(f32[2,256]{1,0:T(2,128)} %copy-done.49) | copy-start | bytes 6148
  249.2 90.3 %copy-start.54 = (f32[768]{0:T(1024)S(1)}, f32[768]{0:T(1024)}, u32[]{:S(2)}) copy-start(f32[768]{0:T(1024)} %param.37) | copy-start | bytes 9220
  249.2 125.6 %all-gather.11.cloned.1.call-start = ((), (), s32[]{:S(2)}) async-start(), calls=%async_computation.10 | async-start | bytes 3932160 | tf_op jit(solution)/shard_map/all_gather | solution.py:220
  302.2 42.1 %copy-start.15 = (bf16[2,256,768]{2,1,0:T(8,128)(2,1)S(1)}, bf16[2,256,768]{2,1,0:T(8,128)(2,1)}, u32[]{:S(2)}) copy-start(bf16[2,256,768]{2,1,0:T(8,128)(2,1)} %param.22) | copy-start | bytes 2359300
  302.2 42.1 %copy-start.41 = (f32[2,256]{1,0:T(2,128)S(1)}, f32[2,256]{1,0:T(2,128)}, u32[]{:S(2)}) copy-start(f32[2,256]{1,0:T(2,128)} %copy-done.40) | copy-start | bytes 6148
  343.1 31.7 %copy-start.27 = (bf16[192,768]{1,0:T(8,128)(2,1)S(1)}, bf16[192,768]{1,0:T(8,128)(2,1)}, u32[]{:S(2)}) copy-start(bf16[192,768]{1,0:T(8,128)(2,1)} %param.30) | copy-start | bytes 884740
  343.1 35.6 %copy-start.45 = (f32[2,256]{1,0:T(2,128)}, f32[2,256]{1,0:T(2,128)S(1)}, u32[]{:S(2)}) copy-start(f32[2,256]{1,0:T(2,128)S(1)} %negate_multiply_fusion.1) | copy-start | bytes 6148
  346.1 151.9 %reduce-scatter.11.cloned.1.call-start = ((), (), s32[]{:S(2)}) async-start(), calls=%async_computation.11 | async-start | bytes 7864320 | tf_op jit(solution)/shard_map/reduce_scatter | solution.py:239
  378.9 6.8 copy-start.3
  382.8 2.9 copy-start.6
  392.6 2.8 copy-start.2
  405.6 6.7 copy-start.3
  409.4 2.9 copy-start.6
  419.2 2.8 copy-start.2
  439.5 7.1 copy-start.62
  439.6 300.9 %all-reduce.6.cloned.1.call-start = ((), (), s32[]{:S(2)}) async-start(), calls=%async_computation.12 | async-start | bytes 14155776 | tf_op jit(solution)/shard_map/psum | solution.py:274
  439.6 7.1 copy-start.59
  446.7 9.4 %copy-start.17 = (bf16[2,1024,768]{2,1,0:T(8,128)(2,1)S(1)}, bf16[2,1024,768]{2,1,0:T(8,128)(2,1)}, u32[]{:S(2)}) copy-start(bf16[2,1024,768]{2,1,0:T(8,128)(2,1)} %all-gather.11.cloned.1.call-done) | copy-start | bytes 9437188
  446.7 9.4 %copy-start.20 = (bf16[2,1024,192]{1,2,0:T(8,128)(2,1)S(1)}, bf16[2,1024,192]{1,2,0:T(8,128)(2,1)}, u32[]{:S(2)}) copy-start(bf16[2,1024,192]{1,2,0:T(8,128)(2,1)} %get-tuple-element.85) | copy-start | bytes 2359300
  446.7 11.1 %copy-start.58 = (bf16[2,1024,768]{2,1,0:T(8,128)(2,1)S(1)}, bf16[2,1024,768]{2,1,0:T(8,128)(2,1)}, u32[]{:S(2)}) copy-start(bf16[2,1024,768]{2,1,0:T(8,128)(2,1)} %all-gather.5.cloned.1.call-done) | copy-start | bytes 9437188
  462.7 37.0 %copy-start.9 = (bf16[2,256,768]{2,1,0:T(8,128)(2,1)S(1)}, bf16[2,256,768]{2,1,0:T(8,128)(2,1)}, u32[]{:S(2)}) copy-start(bf16[2,256,768]{2,1,0:T(8,128)(2,1)} %param.21) | copy-start | bytes 2359300
  462.7 37.0 %copy-start.35 = (f32[2,256]{1,0:T(2,128)S(1)}, f32[2,256]{1,0:T(2,128)}, u32[]{:S(2)}) copy-start(f32[2,256]{1,0:T(2,128)} %copy-done.34) | copy-start | bytes 6148
  462.7 37.0 %copy-start.36 = (f32[768]{0:T(1024)S(1)}, f32[768]{0:T(1024)}, u32[]{:S(2)}) copy-start(f32[768]{0:T(1024)} %param.26) | copy-start | bytes 9220
  462.9 38.7 %copy-start.48 = (f32[2,256]{1,0:T(2,128)S(1)}, f32[2,256]{1,0:T(2,128)}, u32[]{:S(2)}) copy-start(f32[2,256]{1,0:T(2,128)} %copy-done.47) | copy-start | bytes 6148
  462.9 38.7 %copy-start.39 = (f32[2,256]{1,0:T(2,128)S(1)}, f32[2,256]{1,0:T(2,128)}, u32[]{:S(2)}) copy-start(f32[2,256]{1,0:T(2,128)} %copy-done.38) | copy-start | bytes 6148
  487.4 15.0 %copy-start.51 = (f32[768]{0:T(1024)S(1)}, f32[768]{0:T(1024)}, u32[]{:S(2)}) copy-start(f32[768]{0:T(1024)} %get-tuple-element.135) | copy-start | bytes 9220
  487.4 15.0 %copy-start.52 = (f32[768]{0:T(1024)S(1)}, f32[768]{0:T(1024)}, u32[]{:S(2)}) copy-start(f32[768]{0:T(1024)} %get-tuple-element.89) | copy-start | bytes 9220
  487.4 15.0 %copy-start.53 = (f32[768]{0:T(1024)S(1)}, f32[768]{0:T(1024)}, u32[]{:S(2)}) copy-start(f32[768]{0:T(1024)} %get-tuple-element.137) | copy-start | bytes 9220
  487.4 59.3 %copy-start.16 = (bf16[2,256,768]{2,1,0:T(8,128)(2,1)S(1)}, bf16[2,256,768]{2,1,0:T(8,128)(2,1)}, u32[]{:S(2)}) copy-start(bf16[2,256,768]{2,1,0:T(8,128)(2,1)} %param.22) | copy-start | bytes 2359300
  487.4 59.3 %copy-start.42 = (f32[2,256]{1,0:T(2,128)S(1)}, f32[2,256]{1,0:T(2,128)}, u32[]{:S(2)}) copy-start(f32[2,256]{1,0:T(2,128)} %copy-done.40) | copy-start | bytes 6148
  487.4 59.3 %copy-start.46 = (f32[2,256]{1,0:T(2,128)S(1)}, f32[2,256]{1,0:T(2,128)}, u32[]{:S(2)}) copy-start(f32[2,256]{1,0:T(2,128)} %copy-done.45) | copy-start | bytes 6148
  498.1 3.5 copy-start.10
  740.5 3.0 copy-start.26
  740.5 3.8 copy-start.22
  744.3 2.8 copy-start.1
  (43 other events, 62.2 us)
Sparse Core Ops, SparseCore 0:
  13.9 31.2 all-gather.4
  80.7 58.3 reduce-scatter.4
  144.7 28.9 all-gather.6
  194.1 29.4 all-gather.8
  240.7 58.3 reduce-scatter.8
  301.5 37.9 reduce-scatter.6
  346.2 28.5 all-gather.10
  439.7 58.3 reduce-scatter.10
  503.7 236.7 all-reduce.5
where the time goes:
time: 764 us; the launch traced here: 754 us
  waiting for transfers between devices  423 us (55%)
  matrix products  114 us (15%)
  blocking collectives  113 us (15%)
  other arithmetic  57.3 us (8%)
  local copies, waits for them, and re-layouts  29.4 us (4%)
  between operations  15.9 us (2%)
    psum x1, waiting for transfers between devices, local(): lax.psum((qkv_weight_grad, qkv_bias_grad, out_weight_grad, fc_weight_grad...  191 us
    reduce_scatter x1, waiting for transfers between devices, local(): lax.psum_scatter(jnp.einsum('rlh,hd->lrd', part_rows, out_weight, preferr...  58.1 us
    reduce_scatter x1, waiting for transfers between devices, local(): lax.psum_scatter(jnp.einsum('rlf,df->lrd', part_rows, fc_weight, preferre...  49.8 us
    psum x1, blocking collectives, local(): lax.psum((norm1_gain_grad, norm1_shift_grad, norm2_gain_grad, norm2_shift...  44.3 us
    psum x1, blocking collectives, local(): lax.psum((replay_local, fresh_local), ('dp', 'tp'))  39.8 us
    reduce_scatter x1, waiting for transfers between devices, local(): lax.psum_scatter(jnp.einsum('rlf,fd->lrd', part_rows, proj_weight, prefer...  37.3 us
    all_gather x1, waiting for transfers between devices, local(): full_attn_grad = lax.all_gather(attn_low, 'tp', axis=1, tiled=True)  28.6 us
    all_gather x1, waiting for transfers between devices, local(): lax.all_gather(normed_low, 'tp', axis=1, tiled=True)  25.2 us
  transfers between devices with their start and end apart: 9, of which 8 were waited for; matrix products, arithmetic and copies ran while one was open for 8% of the time, Pallas kernels for 0%

commit v1 on v0

v1 whole, which is shorter than its diff:
```python
import functools

import jax
import jax.numpy as jnp
from jax import lax
from jax.experimental import pallas as pl
from jax.experimental.pallas import tpu as pltpu
from jax.sharding import PartitionSpec as P

HD = 64
EPSILON = 1e-05
SCALE = HD ** (-0.5)
EXP2_SCALE = SCALE * 1.4426950408889634
BLOCK = 256
F32 = jnp.float32
BF16 = jnp.bfloat16
NN = (((1,), (0,)), ((), ()))
NT = (((1,), (1,)), ((), ()))
TN = (((0,), (0,)), ((), ()))


def dot(a, b, dims=NN):
    return lax.dot_general(a, b, dims, preferred_element_type=F32)


def layer_norm(values, gain, shift):
    average = jnp.mean(values, axis=-1, keepdims=True)
    centered = values - average
    spread = jnp.mean(centered * centered, axis=-1, keepdims=True)
    return centered * lax.rsqrt(spread + EPSILON) * gain + shift


def smooth_gelu(values):
    return (
        0.5
        * values
        * (1.0 + jnp.tanh(0.7978845608028654 * (values + 0.044715 * values * values * values)))
    )


def attend_kernel(q_ref, k_ref, v_ref, seg_col_ref, seg_row_ref, p_ref, o_ref, inv_ref):
    heads, length, _ = q_ref.shape

    def head(h, _):
        for start in range(0, length, BLOCK):
            stop = start + BLOCK
            rows = slice(start, stop)
            scores = dot(q_ref[h, rows, :], k_ref[h, :stop, :], NT) * EXP2_SCALE
            query_at = start + lax.broadcasted_iota(jnp.int32, (BLOCK, stop), 0)
            key_at = lax.broadcasted_iota(jnp.int32, (BLOCK, stop), 1)
            allowed = (key_at <= query_at) & (seg_col_ref[rows, :] == seg_row_ref[:, :stop])
            scores = jnp.where(allowed, scores, -1e30)
            top = jnp.max(scores, axis=1, keepdims=True)
            exponent = jnp.exp2(scores - top)
            inverse = 1.0 / jnp.sum(exponent, axis=1, keepdims=True)
            low = exponent.astype(BF16)
            p_ref[h, rows, :stop] = low
            inv_ref[h, rows, :] = inverse
            o_ref[h, rows, :] = (dot(low, v_ref[h, :stop, :]) * inverse).astype(BF16)
        return 0

    lax.fori_loop(0, heads, head, 0)


def attend_back_kernel(
    q_ref, k_ref, v_ref, p_ref, o_ref, inv_ref, do_ref, dq_ref, dk_ref, dv_ref, key_acc, value_acc
):
    heads, length, _ = q_ref.shape

    def head(h, _):
        query_t = q_ref[h].T
        for start in range(0, length, BLOCK):
            stop = start + BLOCK
            rows = slice(start, stop)
            weights = p_ref[h, rows, :stop]
            upstream = (do_ref[h, rows, :] * inv_ref[h, rows, :]).astype(BF16)
            row_dot = jnp.sum(
                upstream.astype(F32) * o_ref[h, rows, :].astype(F32), axis=1, keepdims=True
            )
            weight_grad = dot(upstream, v_ref[h, :stop, :], NT)
            score_grad = (weights.astype(F32) * (weight_grad - row_dot)).astype(BF16)
            dq_ref[h, rows, :] = (dot(score_grad, k_ref[h, :stop, :]) * SCALE).astype(BF16)
            key_part = dot(query_t[:, rows], score_grad)
            value_part = dot(upstream.T, weights)
            if start:
                key_acc[:, :start] += key_part[:, :start]
                value_acc[:, :start] += value_part[:, :start]
            key_acc[:, rows] = key_part[:, start:]
            value_acc[:, rows] = value_part[:, start:]
        dk_ref[h] = (key_acc[...] * SCALE).T.astype(BF16)
        dv_ref[h] = value_acc[...].T.astype(BF16)
        return 0

    lax.fori_loop(0, heads, head, 0)


VMEM = pl.BlockSpec(memory_space=pltpu.VMEM)


def attend(q, k, v, segments):
    heads, length, _ = q.shape
    return pl.pallas_call(
        attend_kernel,
        out_shape=(
            jax.ShapeDtypeStruct((heads, length, length), BF16),
            jax.ShapeDtypeStruct((heads, length, HD), BF16),
            jax.ShapeDtypeStruct((heads, length, 1), F32),
        ),
        in_specs=[VMEM] * 5,
        out_specs=(VMEM,) * 3,
        compiler_params=pltpu.CompilerParams(vmem_limit_bytes=56 << 20),
    )(q, k, v, segments[:, None], segments[None, :])


def attend_back(q, k, v, p, o, inverse, upstream):
    heads, length, _ = q.shape
    shape = jax.ShapeDtypeStruct((heads, length, HD), BF16)
    return pl.pallas_call(
        attend_back_kernel,
        out_shape=(shape,) * 3,
        in_specs=[VMEM] * 7,
        out_specs=(VMEM,) * 3,
        scratch_shapes=[pltpu.VMEM((HD, length), F32)] * 2,
        compiler_params=pltpu.CompilerParams(vmem_limit_bytes=56 << 20),
    )(q, k, v, p, o, inverse, upstream)


def local(
    tokens,
    cotangent,
    segment_ids,
    valid_mask,
    row_half,
    norm1_gain,
    norm1_shift,
    qkv_weight,
    qkv_bias,
    out_weight,
    out_bias,
    norm2_gain,
    norm2_shift,
    fc_weight,
    fc_bias,
    proj_weight,
    proj_bias,
):
    place = lax.axis_index("tp")
    chip = place // 2
    core = place % 2
    owned, width = tokens.shape[1], tokens.shape[2]
    own_heads = out_weight.shape[0] // HD
    heads = 2 * own_heads

    def swap_chip(value):
        return lax.ppermute(value, "tp", [(i, i ^ 2) for i in range(4)])

    def swap_core(value):
        return lax.ppermute(value, "tp", [(i, i ^ 1) for i in range(4)])

    def row_pair(value):
        keep = jnp.where(chip == 0, value[0], value[1])
        got = swap_chip(jnp.where(chip == 0, value[1], value[0]))
        return jnp.where(chip == 0, jnp.stack([keep, got]), jnp.stack([got, keep]))

    def row_unpair(value):
        keep = jnp.where(chip == 0, value[0], value[1])
        got = swap_chip(jnp.where(chip == 0, value[1], value[0]))
        return jnp.where(chip == 0, jnp.stack([keep, got]), jnp.stack([got, keep]))

    def gather(value):
        other = swap_core(value)
        pairs = jnp.where(
            core == 0, jnp.stack([value, other], 1), jnp.stack([other, value], 1)
        )
        return pairs.reshape((4 * owned,) + value.shape[2:])

    def scatter(value):
        parts = value.reshape(2, 2, owned, width)
        keep = jnp.where(core == 0, parts[:, 0], parts[:, 1])
        give = jnp.where(core == 0, parts[:, 1], parts[:, 0])
        return keep + swap_core(give)

    other_qkv = swap_chip(qkv_weight)
    other_out = swap_chip(out_weight)
    other_fc = swap_chip(fc_weight)
    other_proj = swap_chip(proj_weight)
    qkv_all = jnp.concatenate([qkv_weight, other_qkv], axis=2)
    out_all = jnp.concatenate([out_weight, other_out], axis=0)
    fc_all = jnp.concatenate([fc_weight, other_fc], axis=1)
    proj_all = jnp.concatenate([proj_weight, other_proj], axis=0)
    qkv_bias_all = jnp.concatenate([qkv_bias, swap_chip(qkv_bias)], axis=1)
    fc_bias_all = jnp.concatenate([fc_bias, swap_chip(fc_bias)], axis=0)

    valid_float = valid_mask.astype(F32)
    row_counts = jnp.sum(valid_float, axis=1)
    replay_local = jnp.sum(jnp.where(row_half == 0, row_counts, 0.0))
    fresh_local = jnp.sum(jnp.where(row_half == 1, row_counts, 0.0))
    replay_count, fresh_count = lax.psum((replay_local, fresh_local), ("dp", "tp"))
    row_scale = (replay_count + fresh_count) / (
        2.0 * jnp.where(row_half == 0, replay_count, fresh_count)
    )
    my_scale = jnp.where(chip == 0, row_scale[0], row_scale[1])

    rows = row_pair(tokens).astype(F32)
    segments = gather(row_pair(segment_ids))
    valid = row_pair(valid_float)
    normed, norm1_back = jax.vjp(layer_norm, rows, norm1_gain, norm1_shift)
    full_normed = gather(normed.astype(BF16))
    qkv = jnp.einsum(
        "ld,dchk->chlk",
        full_normed,
        qkv_all.reshape(width, 3, heads, HD),
        preferred_element_type=F32,
    ) + qkv_bias_all.reshape(3, heads, 1, HD)
    qkv_low = qkv.astype(BF16)
    weights, mixed, inverse = attend(qkv_low[0], qkv_low[1], qkv_low[2], segments)
    out_split = out_all.reshape(heads, HD, width)
    attn = scatter(
        jnp.einsum("hlk,hkd->ld", mixed, out_split, preferred_element_type=F32)
    )
    middle = rows + attn + out_bias
    normed_two, norm2_back = jax.vjp(layer_norm, middle, norm2_gain, norm2_shift)
    full_normed_two = gather(normed_two.astype(BF16))
    hidden_pre = jnp.dot(full_normed_two, fc_all, preferred_element_type=F32) + fc_bias_all
    hidden_act, gelu_back = jax.vjp(smooth_gelu, hidden_pre)
    hidden_low = hidden_act.astype(BF16)
    mlp = scatter(jnp.dot(hidden_low, proj_all, preferred_element_type=F32))
    result = middle + mlp + proj_bias
    output = row_unpair(result.astype(BF16))

    out_grad = row_pair(cotangent).astype(F32) * (valid * my_scale)[..., None]
    branch_low = out_grad.astype(BF16)
    proj_bias_grad = jnp.sum(branch_low, axis=(0, 1), dtype=F32)
    full_grad = gather(branch_low)
    hidden_grad = dot(full_grad, proj_all, NT)
    proj_weight_grad = dot(hidden_low, full_grad, TN)
    (pre_grad,) = gelu_back(hidden_grad)
    pre_low = pre_grad.astype(BF16)
    fc_bias_grad = jnp.sum(pre_low, axis=0, dtype=F32)
    fc_weight_grad = dot(full_normed_two, pre_low, TN)
    normed_two_grad = scatter(dot(pre_low, fc_all, NT))
    middle_part, norm2_gain_grad, norm2_shift_grad = norm2_back(normed_two_grad)
    middle_grad = out_grad + middle_part
    attn_low = middle_grad.astype(BF16)
    out_bias_grad = jnp.sum(attn_low, axis=(0, 1), dtype=F32)
    full_attn_grad = gather(attn_low)
    mixed_grad = jnp.einsum("ld,hkd->hlk", full_attn_grad, out_split, preferred_element_type=F32)
    out_weight_grad = jnp.einsum(
        "hlk,ld->hkd", mixed, full_attn_grad, preferred_element_type=F32
    ).reshape(heads * HD, width)
    query_grad, key_grad, value_grad = attend_back(
        qkv_low[0], qkv_low[1], qkv_low[2], weights, mixed, inverse, mixed_grad
    )
    qkv_grad = jnp.stack([query_grad, key_grad, value_grad])
    qkv_bias_grad = jnp.sum(qkv_grad, axis=2, dtype=F32).reshape(3, heads * HD)
    qkv_weight_grad = jnp.einsum(
        "ld,chlk->dchk", full_normed, qkv_grad, preferred_element_type=F32
    ).reshape(width, 3, heads * HD)
    normed_grad = scatter(
        jnp.einsum(
            "chlk,dchk->ld",
            qkv_grad,
            qkv_all.reshape(width, 3, heads, HD),
            preferred_element_type=F32,
        )
    )
    tokens_part, norm1_gain_grad, norm1_shift_grad = norm1_back(normed_grad)
    tokens_grad = row_unpair(middle_grad + tokens_part)

    (
        norm1_gain_grad,
        norm1_shift_grad,
        norm2_gain_grad,
        norm2_shift_grad,
        out_bias_grad,
        proj_bias_grad,
    ) = lax.psum(
        (
            norm1_gain_grad,
            norm1_shift_grad,
            norm2_gain_grad,
            norm2_shift_grad,
            out_bias_grad,
            proj_bias_grad,
        ),
        ("dp", "tp"),
    )

    def reduce_weight(value, axis, low=True):
        size = value.shape[axis] // 2
        mine = lax.slice_in_dim(value, 0, size, axis=axis)
        other = lax.slice_in_dim(value, size, 2 * size, axis=axis)
        if low:
            total = mine + swap_chip(other.astype(BF16)).astype(F32)
            return lax.psum(total.astype(BF16), "dp").astype(F32)
        return lax.psum(mine + swap_chip(other), "dp")

    return (
        output,
        tokens_grad,
        norm1_gain_grad,
        norm1_shift_grad,
        reduce_weight(qkv_weight_grad, 2),
        reduce_weight(qkv_bias_grad, 1, False),
        reduce_weight(out_weight_grad, 0),
        out_bias_grad,
        norm2_gain_grad,
        norm2_shift_grad,
        reduce_weight(fc_weight_grad, 1),
        reduce_weight(fc_bias_grad, 0, False),
        reduce_weight(proj_weight_grad, 0),
        proj_bias_grad,
    )


def solution(mesh):
    in_specs = (
        P("dp", "tp", None),
        P("dp", "tp", None),
        P("dp", "tp"),
        P("dp", "tp"),
        P("dp"),
        P(),
        P(),
        P(None, None, "tp"),
        P(None, "tp"),
        P("tp", None),
        P(),
        P(),
        P(),
        P(None, "tp"),
        P("tp"),
        P("tp", None),
        P(),
    )
    out_specs = (
        P("dp", "tp", None),
        P("dp", "tp", None),
        P(),
        P(),
        P(None, None, "tp"),
        P(None, "tp"),
        P("tp", None),
        P(),
        P(),
        P(),
        P(None, "tp"),
        P("tp"),
        P("tp", None),
        P(),
    )
    return jax.shard_map(local, mesh=mesh, in_specs=in_specs, out_specs=out_specs, check_vma=False)
```

time: 764 us -> 493 us (0.65)
  waiting for transfers between devices: 423 us -> 128 us
  matrix products: 114 us -> 40.3 us
  blocking collectives: 113 us -> 153 us
  Pallas kernels: 0 us -> 39.7 us
  starting transfers between devices: 0.72 us -> 26.4 us
  other arithmetic: 57.3 us -> 48.2 us
    reduce_scatter x4 -> x0, waiting for transfers between devices: 156 us -> none  [the longest x1 58.1 us: local(): lax.psum_scatter(jnp.einsum('rlh,hd->lrd', part_rows, out_weight, preferr...]
    psum x1, waiting for transfers between devices: 191 us -> 41.5 us  [reduce_weight(): return lax.psum(total.astype(BF16), 'dp').astype(F32)]
    ppermute x0 -> x27, waiting for transfers between devices: none -> 87 us  [the longest x18 86.9 us: swap_chip(): return lax.ppermute(value, 'tp', [(i, i ^ 2) for i in range(4)])]
    all_gather x4 -> x0, waiting for transfers between devices: 75.8 us -> none  [the longest x1 28.6 us: local(): full_attn_grad = lax.all_gather(attn_low, 'tp', axis=1, tiled=True)]
    dot_general x40 -> x12, matrix products: 114 us -> 40.3 us  [the longest x4 17.5 us: dot(): return lax.dot_general(a, b, dims, preferred_element_type=F32)]
    psum x1, blocking collectives: 39.8 us -> 93.2 us  [local(): lax.psum((replay_local, fresh_local), ('dp', 'tp'))]
    pallas_call x0 -> x2, Pallas kernels: none -> 39.7 us  [the longest x1 19.9 us: attend(): pl.pallas_call(attend_kernel, out_shape=(jax.ShapeDtypeStruct((heads, len...]
    ppermute x0 -> x27, starting transfers between devices: none -> 26.4 us  [the longest x18 24.6 us: swap_chip(): return lax.ppermute(value, 'tp', [(i, i ^ 2) for i in range(4)])]
  transfers between devices with their start and end apart: 9 -> 28, of which waited for: 8 -> 9; matrix products, arithmetic and copies ran while one was open for 8% -> 16% of each run, Pallas kernels for 0% -> 4%
where the time goes in v1:
time: 493 us; the launch traced here: 486 us
  blocking collectives  153 us (31%)
  waiting for transfers between devices  128 us (26%)
  other arithmetic  48.2 us (10%)
  matrix products  40.3 us (8%)
  Pallas kernels  39.7 us (8%)
  local copies, waits for them, and re-layouts  32.3 us (7%)
  starting transfers between devices  26.4 us (5%)
  between operations  17.8 us (4%)
    psum x1, blocking collectives, local(): lax.psum((replay_local, fresh_local), ('dp', 'tp'))  93.2 us
    ppermute x18, waiting for transfers between devices, swap_chip(): return lax.ppermute(value, 'tp', [(i, i ^ 2) for i in range(4)])  86.9 us
    psum x1, waiting for transfers between devices, reduce_weight(): return lax.psum(total.astype(BF16), 'dp').astype(F32)  41.5 us
    psum x1, blocking collectives, local(): lax.psum((norm1_gain_grad, norm1_shift_grad, norm2_gain_grad, norm2_shift...  38.6 us
    ppermute x18, starting transfers between devices, swap_chip(): return lax.ppermute(value, 'tp', [(i, i ^ 2) for i in range(4)])  24.6 us
    psum x1, blocking collectives, reduce_weight(): return lax.psum(mine + swap_chip(other), 'dp')  20.7 us
    pallas_call x1, Pallas kernels, attend(): pl.pallas_call(attend_kernel, out_shape=(jax.ShapeDtypeStruct((heads, len...  19.9 us
    pallas_call x1, Pallas kernels, attend_back(): pl.pallas_call(attend_back_kernel, out_shape=(shape,) * 3, in_specs=[VMEM...  19.8 us
  transfers between devices with their start and end apart: 28, of which 9 were waited for; matrix products, arithmetic and copies ran while one was open for 16% of the time, Pallas kernels for 4%

profile of v1, /device:TPU:0, one launch (start us, length us, event | category | flops | bytes accessed | tf_op | source)
XLA Modules:
  0.0 485.7 jit_solution(11338708302863639797)
XLA Ops:
  8.5 3.0 collective-permute-start
  11.7 2.0 collective-permute-start.3
  13.7 1.9 collective-permute-start.1
  16.6 1.7 constant_dynamic-update-slice_fusion.3
  18.3 3.2 collective-permute-done.4
  25.7 2.3 collective-permute-done.6
  28.0 1.7 constant_dynamic-update-slice_fusion.2
  30.1 15.9 %collective-permute-done.1 = bf16[768,3,192]{0,2,1:T(8,128)(2,1)S(1)} collective-permute-done((bf16[768,3,192]{0,2,1:T(8,128)(2,1)S(1)}, bf16[768,3,192]{0,2,1:T(8,128)(2,1)S(1)}, u32[]{:S(2)}, u32[]{:S(2)}) %collective-permute-start.1) | collective-permute-done | bytes 884768 | tf_op jit(solution)/shard_map/ppermute | solution.py:155
  46.1 2.3 maximum_select_fusion
  49.6 4.0 fusion.6
  53.7 2.4 slice_bitcast_fusion.6
  56.1 19.9 %shard_map.272 = (bf16[6,1024,1024]{2,1,0:T(8,128)(2,1)}, bf16[6,1024,64]{2,1,0:T(8,128)(2,1)}, f32[6,1024,1]{2,1,0:T(8,128)}) custom-call(bf16[6,1024,64]{2,1,0:T(8,128)(2,1)} %get-tuple-element.66.q_ref, bf16[6,1024,64]{2,1,0:T(8,128)(2,1)} %get-tuple-element.65.k_ref, bf16[6,1024,64]{2,1,0:T(8,128)(2,1)} %get-tuple-element.64.v_ref, ...), custom_call_target="tpu_custom_call" | custom-call | tf_op jit(solution)/shard_map/pallas_call | solution.py:102
  76.0 2.4 fusion.26
  81.6 1.7 collective-permute-start.15
  83.8 1.7 collective-permute-start.9
  86.5 93.2 %all-reduce.1 = (f32[]{:T(128)}, f32[]{:T(128)}) all-reduce(f32[]{:T(128)} %get-tuple-element.34, f32[]{:T(128)} %get-tuple-element.33), channel_id=1, replica_groups=mesh['dp'=8,'tp'=4] {'dp','tp'}, use_global_device_ids=true, to_apply=%region_8.9 | all-reduce | flops 2 | bytes 16 | tf_op jit(solution)/shard_map/psum | solution.py:198
  181.0 2.4 constant_dynamic-update-slice_fusion.5
  183.4 2.0 fusion.37
  185.4 2.4 constant_dynamic-update-slice_fusion.7
  189.6 2.3 collective-permute-start.10
  195.3 2.9 fusion.44
  205.4 2.6 fusion.47
  208.0 9.5 %convert_reduce_fusion.1 = (f32[1536]{0:T(1024)}, bf16[1024,1536]{1,0:T(8,128)(2,1)S(1)}, bf16[1024,1536]{1,0:T(8,128)(2,1)S(1)}) fusion(f32[1024,1536]{1,0:T(8,128)S(1)} %fusion.47, f32[1536]{0:T(1024)S(1)} %pad_maximum_fusion.1, bf16[1024,768]{1,0:T(8,128)(2,1)S(1)} %bitcast.231, bf16[1536,768]{1,0:T(8,128)(2,1)S(1)} %constant_dynamic-update-slice_fusion.6), kind=kOutput, calls=%fused_computation.12 | convolution fusion | flops 2461530624 | bytes 16527360 | tf_op jit(solution)/shard_map/dot_general | solution.py:23
  217.5 2.6 fusion.49
  220.4 2.6 fusion.48
  223.7 2.6 fusion.52
  226.6 2.1 collective-permute-start.24
  230.1 1.7 fusion.43
  232.8 2.8 fusion.53
  236.9 18.5 %collective-permute-done.24 = bf16[768,768]{1,0:T(8,128)(2,1)S(1)} collective-permute-done((bf16[768,768]{1,0:T(8,128)(2,1)S(1)}, bf16[768,768]{1,0:T(8,128)(2,1)S(1)}, u32[]{:S(2)}, u32[]{:S(2)}) %collective-permute-start.24) | collective-permute-done | bytes 1179680 | tf_op jit(solution)/shard_map/ppermute | solution.py:155
  257.9 3.4 convolution_bitcast_fusion.1.do_ref
  261.3 19.8 %shard_map.273 = (bf16[6,1024,64]{2,1,0:T(8,128)(2,1)}, bf16[6,1024,64]{2,1,0:T(8,128)(2,1)}, bf16[6,1024,64]{2,1,0:T(8,128)(2,1)}) custom-call(bf16[6,1024,64]{2,1,0:T(8,128)(2,1)} %get-tuple-element.66.q_ref, bf16[6,1024,64]{2,1,0:T(8,128)(2,1)} %get-tuple-element.65.k_ref, bf16[6,1024,64]{2,1,0:T(8,128)(2,1)} %get-tuple-element.64.v_ref, ...), custom_call_target="tpu_custom_call" | custom-call | tf_op jit(solution)/shard_map/pallas_call | solution.py:118
  281.1 3.9 convert_reduce_fusion
  285.0 2.4 convolution_bitcast_fusion
  289.6 6.0 %copy.69 = bf16[3,6,64,1024]{3,2,1,0:T(8,128)(2,1)} copy(bf16[3,6,64,1024]{2,3,1,0:T(8,128)(2,1)} %bitcast.205) | data formatting | bytes 4718592 | tf_op jit(solution)/shard_map/ld,chlk->dchk/dot_general | solution.py:256
  295.6 4.4 fusion.50
  300.2 2.1 collective-permute-start.21
  304.5 2.6 fusion.11
  307.2 21.7 %collective-permute-done.23 = bf16[192,768]{1,0:T(8,128)(2,1)S(1)} collective-permute-done((bf16[192,768]{1,0:T(8,128)(2,1)S(1)}, bf16[192,768]{1,0:T(8,128)(2,1)S(1)}, u32[]{:S(2)}, u32[]{:S(2)}) %collective-permute-start.23) | collective-permute-done | bytes 294944 | tf_op jit(solution)/shard_map/ppermute | solution.py:155
  330.9 3.6 fusion.39
  336.9 1.8 collective-permute-start.20
  341.7 23.2 %collective-permute-done.25 = f32[768]{0:T(1024)S(1)} collective-permute-done((f32[768]{0:T(1024)S(1)}, f32[768]{0:T(1024)S(1)}, u32[]{:S(2)}, u32[]{:S(2)}) %collective-permute-start.25) | collective-permute-done | bytes 3104 | tf_op jit(solution)/shard_map/ppermute | solution.py:155
  368.6 20.7 %all-reduce.2 = (f32[3,192]{1,0:T(4,128)}, f32[768]{0:T(1024)}) all-reduce(f32[3,192]{1,0:T(4,128)S(1)} %slice_add_fusion.4, f32[768]{0:T(1024)S(1)} %slice_add_fusion.3), channel_id=1, replica_groups=mesh['dp'=8,'tp'=4] {'dp'}, use_global_device_ids=true, to_apply=%region_19.20 | all-reduce | flops 1344 | bytes 10752 | tf_op jit(solution)/shard_map/psum | solution.py:296
  389.4 38.6 %all-reduce = (f32[768]{0:T(1024)}, f32[768]{0:T(1024)}, f32[768]{0:T(1024)}, f32[768]{0:T(1024)}, f32[768]{0:T(1024)}, /*index=5*/f32[768]{0:T(1024)}) all-reduce(f32[768]{0:T(1024)S(1)} %copy-done.33, f32[768]{0:T(1024)S(1)} %copy-done.32, f32[768]{0:T(1024)S(1)} %copy-done.31, ...), channel_id=1, replica_groups=mesh['dp'=8,'tp'=4] {'dp','tp'}, use_global_device_ids=true, to_apply=%region_14.15 | all-reduce | flops 4608 | bytes 36864 | tf_op jit(solution)/shard_map/psum | solution.py:277
  429.3 41.5 %all-reduce.6.cloned.1.call-done = (bf16[768,3,192]{0,2,1:T(8,128)(2,1)}, bf16[192,768]{1,0:T(8,128)(2,1)}, bf16[768,768]{1,0:T(8,128)(2,1)}, bf16[768,768]{1,0:T(8,128)(2,1)}) async-done(((bf16[768,3,192]{0,2,1:T(8,128)(2,1)}, bf16[192,768]{1,0:T(8,128)(2,1)}, bf16[768,768]{1,0:T(8,128)(2,1)}, bf16[768,768]{1,0:T(8,128)(2,1)}), (bf16[768,3,192]{0,2,1:T(8,128)(2,1)}, bf16[192,768]{1,0:T(8,128)(2,1)}, ...) | async-done | bytes 3538960 | tf_op jit(solution)/shard_map/psum | solution.py:295
  470.7 1.9 convert_element_type.150
  472.6 2.5 convert_element_type.145
  475.2 1.6 convert_element_type.154
  (198 shorter events, 49.8 us)
Async XLA Ops:
  7.2 4.5 copy-start.37
  7.2 6.5 %copy-start.12 = (bf16[768,3,192]{0,2,1:T(8,128)(2,1)S(1)}, bf16[768,3,192]{0,2,1:T(8,128)(2,1)}, u32[]{:S(2)}) copy-start(bf16[768,3,192]{0,2,1:T(8,128)(2,1)} %param.24) | copy-start | bytes 2654212
  7.2 463.5 %all-reduce.6.cloned.1.call-start = ((), (), s32[]{:S(2)}) async-start(), calls=%async_computation | async-start | bytes 7077888 | tf_op jit(solution)/shard_map/psum | solution.py:295
  8.5 9.8 %copy-start.35 = (s32[2,256]{1,0:T(2,128)S(1)}, s32[2,256]{1,0:T(2,128)}, u32[]{:S(2)}) copy-start(s32[2,256]{1,0:T(2,128)} %param.20) | copy-start | bytes 6148
  8.5 13.0 %collective-permute-start = (bf16[256,768]{1,0:T(8,128)(2,1)S(1)}, bf16[256,768]{1,0:T(8,128)(2,1)S(1)}, u32[]{:S(2)}, u32[]{:S(2)}) collective-permute-start(bf16[256,768]{1,0:T(8,128)(2,1)S(1)} %get-tuple-element.74), channel_id=1, source_target_pairs={{0,2},{1,3},{2,0},{3,1},{4,6},{5,7},{6,4},{7,5},{8,10},{9,11},{10,... | collective-permute-start | bytes 1179656 | tf_op jit(solution)/shard_map/ppermute | solution.py:155
  11.5 11.3 %copy-start.21 = (f32[768]{0:T(1024)S(1)}, f32[768]{0:T(1024)}, u32[]{:S(2)}) copy-start(f32[768]{0:T(1024)} %param.22) | copy-start | bytes 9220
  11.5 11.3 %copy-start.26 = (f32[768]{0:T(1024)S(1)}, f32[768]{0:T(1024)}, u32[]{:S(2)}) copy-start(f32[768]{0:T(1024)} %param.23) | copy-start | bytes 9220
  11.6 10.0 %collective-permute-start.4 = (s32[256]{0:T(256)S(1)}, s32[256]{0:T(256)S(1)}, u32[]{:S(2)}, u32[]{:S(2)}) collective-permute-start(s32[256]{0:T(256)S(1)} %bitcast.249), channel_id=1, source_target_pairs={{0,2},{1,3},{2,0},{3,1},{4,6},{5,7},{6,4},{7,5},{8,10},{9,11},{10,... | collective-permute-start | bytes 3080 | tf_op jit(solution)/shard_map/ppermute | solution.py:155
  11.7 12.2 %collective-permute-start.3 = (f32[3,192]{1,0:T(4,128)S(1)}, f32[3,192]{1,0:T(4,128)S(1)}, u32[]{:S(2)}, u32[]{:S(2)}) collective-permute-start(f32[3,192]{1,0:T(4,128)S(1)} %copy-done.37), channel_id=1, source_target_pairs={{0,2},{1,3},{2,0},{3,1},{4,6},{5,7},{6,4},{7,5},{8,10},{9,11},{10,... | collective-permute-start | bytes 6920 | tf_op jit(solution)/shard_map/ppermute | solution.py:155
  13.7 14.4 %collective-permute-start.6 = (bf16[192,768]{1,0:T(8,128)(2,1)}, bf16[192,768]{1,0:T(8,128)(2,1)}, u32[]{:S(2)}, u32[]{:S(2)}) collective-permute-start(bf16[192,768]{1,0:T(8,128)(2,1)} %param.26), channel_id=1, source_target_pairs={{0,2},{1,3},{2,0},{3,1},{4,6},{5,7},{6,4},{7,5},{8,10},{9,11},{10,... | collective-permute-start | bytes 884744 | tf_op jit(solution)/shard_map/ppermute | solution.py:155
  13.7 32.3 %collective-permute-start.1 = (bf16[768,3,192]{0,2,1:T(8,128)(2,1)S(1)}, bf16[768,3,192]{0,2,1:T(8,128)(2,1)S(1)}, u32[]{:S(2)}, u32[]{:S(2)}) collective-permute-start(bf16[768,3,192]{0,2,1:T(8,128)(2,1)S(1)} %copy-done.12), channel_id=1, source_target_pairs={{0,2},{1,3},{2,0},{3,1},{4,6},{5,7},{6,4},{7,5},{8,10},{9,11},{10,... | collective-permute-start | bytes 2654216 | tf_op jit(solution)/shard_map/ppermute | solution.py:155
  21.5 2.4 collective-permute-start.5
  23.2 22.9 %collective-permute-start.2 = (bf16[2,256,768]{2,1,0:T(8,128)(2,1)S(1)}, bf16[2,256,768]{2,1,0:T(8,128)(2,1)}, u32[]{:S(2)}, u32[]{:S(2)}) collective-permute-start(bf16[2,256,768]{2,1,0:T(8,128)(2,1)S(1)} %fusion.17), channel_id=1, source_target_pairs={{0,1},{1,0},{2,3},{3,2},{4,5},{5,4},{6,7},{7,6},{8,9},{9,8},{10,11... | collective-permute-start | bytes 2359304 | tf_op jit(solution)/shard_map/ppermute | solution.py:158
  25.7 20.3 %copy-start.16 = (bf16[768,3,384]{0,2,1:T(8,128)(2,1)S(1)}, bf16[768,3,384]{0,2,1:T(8,128)(2,1)}, u32[]{:S(2)}) copy-start(bf16[768,3,384]{0,2,1:T(8,128)(2,1)} %constant_dynamic-update-slice_fusion.1) | copy-start | bytes 5308420
  56.1 19.9 %copy-start.19 = (bf16[384,768]{1,0:T(8,128)(2,1)S(1)}, bf16[384,768]{1,0:T(8,128)(2,1)}, u32[]{:S(2)}) copy-start(bf16[384,768]{1,0:T(8,128)(2,1)} %constant_dynamic-update-slice_fusion.2) | copy-start | bytes 1769476
  81.0 4.9 %copy-start.39 = (s32[2]{0:T(128)S(1)}, s32[2]{0:T(128)}, u32[]{:S(2)}) copy-start(s32[2]{0:T(128)} %param.21) | copy-start | bytes 28
  81.0 114.3 %collective-permute-start.7 = (f32[2,256,768]{2,1,0:T(8,128)S(1)}, f32[2,256,768]{2,1,0:T(8,128)}, u32[]{:S(2)}, u32[]{:S(2)}) collective-permute-start(f32[2,256,768]{2,1,0:T(8,128)S(1)} %fusion.25), channel_id=1, source_target_pairs={{0,1},{1,0},{2,3},{3,2},{4,5},{5,4},{6,7},{7,6},{8,9},{9,8},{10,11... | collective-permute-start | bytes 4718600 | tf_op jit(solution)/shard_map/ppermute | solution.py:158
  81.6 108.0 %collective-permute-start.15 = (f32[256]{0:T(256)}, f32[256]{0:T(256)}, u32[]{:S(2)}, u32[]{:S(2)}) collective-permute-start(f32[256]{0:T(256)} %bitcast.41), channel_id=1, source_target_pairs={{0,2},{1,3},{2,0},{3,1},{4,6},{5,7},{6,4},{7,5},{8,10},{9,11},{10,... | collective-permute-start | bytes 3080 | tf_op jit(solution)/shard_map/ppermute | solution.py:155
  83.4 111.1 %collective-permute-start.14 = (bf16[256,768]{1,0:T(8,128)(2,1)S(1)}, bf16[256,768]{1,0:T(8,128)(2,1)S(1)}, u32[]{:S(2)}, u32[]{:S(2)}) collective-permute-start(bf16[256,768]{1,0:T(8,128)(2,1)S(1)} %get-tuple-element.70), channel_id=1, source_target_pairs={{0,2},{1,3},{2,0},{3,1},{4,6},{5,7},{6,4},{7,5},{8,10},{9,11},{10,... | collective-permute-start | bytes 1179656 | tf_op jit(solution)/shard_map/ppermute | solution.py:155
  83.8 116.7 %collective-permute-start.9 = (bf16[768,768]{1,0:T(8,128)(2,1)}, bf16[768,768]{1,0:T(8,128)(2,1)}, u32[]{:S(2)}, u32[]{:S(2)}) collective-permute-start(bf16[768,768]{1,0:T(8,128)(2,1)} %param.30), channel_id=1, source_target_pairs={{0,2},{1,3},{2,0},{3,1},{4,6},{5,7},{6,4},{7,5},{8,10},{9,11},{10,... | collective-permute-start | bytes 3538952 | tf_op jit(solution)/shard_map/ppermute | solution.py:155
  85.5 117.8 %collective-permute-start.11 = (bf16[768,768]{1,0:T(8,128)(2,1)}, bf16[768,768]{1,0:T(8,128)(2,1)}, u32[]{:S(2)}, u32[]{:S(2)}) collective-permute-start(bf16[768,768]{1,0:T(8,128)(2,1)} %param.32), channel_id=1, source_target_pairs={{0,2},{1,3},{2,0},{3,1},{4,6},{5,7},{6,4},{7,5},{8,10},{9,11},{10,... | collective-permute-start | bytes 3538952 | tf_op jit(solution)/shard_map/ppermute | solution.py:155
  189.6 4.1 collective-permute-start.10
  195.3 4.7 collective-permute-start.16
  199.2 5.8 %collective-permute-start.8 = (bf16[2,256,768]{2,1,0:T(8,128)(2,1)S(1)}, bf16[2,256,768]{2,1,0:T(8,128)(2,1)S(1)}, u32[]{:S(2)}, u32[]{:S(2)}) collective-permute-start(bf16[2,256,768]{2,1,0:T(8,128)(2,1)S(1)} %add_convert_fusion.1), channel_id=1, source_target_pairs={{0,1},{1,0},{2,3},{3,2},{4,5},{5,4},{6,7},{7,6},{8,9},{9,8},{10,11... | collective-permute-start | bytes 2359304 | tf_op jit(solution)/shard_map/ppermute | solution.py:158
  220.3 8.4 %collective-permute-start.17 = (f32[2,256,768]{2,1,0:T(8,128)S(1)}, f32[2,256,768]{2,1,0:T(8,128)S(1)}, u32[]{:S(2)}, u32[]{:S(2)}) collective-permute-start(f32[2,256,768]{2,1,0:T(8,128)S(1)} %select_bitcast_fusion.1), channel_id=1, source_target_pairs={{0,1},{1,0},{2,3},{3,2},{4,5},{5,4},{6,7},{7,6},{8,9},{9,8},{10,11... | collective-permute-start | bytes 4718600 | tf_op jit(solution)/shard_map/ppermute | solution.py:158
  223.2 6.9 %collective-permute-start.12 = (f32[2,256,768]{2,1,0:T(8,128)S(1)}, f32[2,256,768]{2,1,0:T(8,128)S(1)}, u32[]{:S(2)}, u32[]{:S(2)}) collective-permute-start(f32[2,256,768]{2,1,0:T(8,128)S(1)} %select_bitcast_fusion.2), channel_id=1, source_target_pairs={{0,1},{1,0},{2,3},{3,2},{4,5},{5,4},{6,7},{7,6},{8,9},{9,8},{10,11... | collective-permute-start | bytes 4718600 | tf_op jit(solution)/shard_map/ppermute | solution.py:158
  226.6 28.9 %collective-permute-start.24 = (bf16[768,768]{1,0:T(8,128)(2,1)S(1)}, bf16[768,768]{1,0:T(8,128)(2,1)S(1)}, u32[]{:S(2)}, u32[]{:S(2)}) collective-permute-start(bf16[768,768]{1,0:T(8,128)(2,1)S(1)} %slice.286), channel_id=1, source_target_pairs={{0,2},{1,3},{2,0},{3,1},{4,6},{5,7},{6,4},{7,5},{8,10},{9,11},{10,... | collective-permute-start | bytes 3538952 | tf_op jit(solution)/shard_map/ppermute | solution.py:155
  232.8 24.1 %collective-permute-start.18 = (bf16[2,256,768]{2,1,0:T(8,128)(2,1)S(1)}, bf16[2,256,768]{2,1,0:T(8,128)(2,1)S(1)}, u32[]{:S(2)}, u32[]{:S(2)}) collective-permute-start(bf16[2,256,768]{2,1,0:T(8,128)(2,1)S(1)} %get-tuple-element.56), channel_id=1, source_target_pairs={{0,1},{1,0},{2,3},{3,2},{4,5},{5,4},{6,7},{7,6},{8,9},{9,8},{10,11... | collective-permute-start | bytes 2359304 | tf_op jit(solution)/shard_map/ppermute | solution.py:158
  235.6 21.3 %copy-start.8 = (f32[1536,768]{1,0:T(8,128)}, f32[1536,768]{1,0:T(8,128)S(1)}, u32[]{:S(2)}) copy-start(f32[1536,768]{1,0:T(8,128)S(1)} %fusion.53) | copy-start | bytes 14155780
  236.8 67.7 %collective-permute-start.26 = (bf16[768,768]{1,0:T(8,128)(2,1)}, bf16[768,768]{1,0:T(8,128)(2,1)}, u32[]{:S(2)}, u32[]{:S(2)}) collective-permute-start(bf16[768,768]{1,0:T(8,128)(2,1)} %slice.285), channel_id=1, source_target_pairs={{0,2},{1,3},{2,0},{3,1},{4,6},{5,7},{6,4},{7,5},{8,10},{9,11},{10,... | collective-permute-start | bytes 3538952 | tf_op jit(solution)/shard_map/ppermute | solution.py:155
  289.6 41.2 %collective-permute-start.19 = (f32[2,256,768]{2,1,0:T(8,128)}, f32[2,256,768]{2,1,0:T(8,128)}, u32[]{:S(2)}, u32[]{:S(2)}) collective-permute-start(f32[2,256,768]{2,1,0:T(8,128)} %select_bitcast_fusion), channel_id=1, source_target_pairs={{0,1},{1,0},{2,3},{3,2},{4,5},{5,4},{6,7},{7,6},{8,9},{9,8},{10,11... | collective-permute-start | bytes 4718600 | tf_op jit(solution)/shard_map/ppermute | solution.py:158
  295.6 8.9 %slice-start = ((s8[4718592]{0:T(1024)(128)(4,1)}), s8[4194304]{0:T(1024)(128)(4,1)S(1)}, s32[]{:S(2)}) async-start(s8[4718592]{0:T(1024)(128)(4,1)} %bitcast.225), calls=%async_computation.1 | async-start | bytes 8388608
  295.6 6.7 %copy-start.6 = (bf16[2,2,256,768]{3,2,1,0:T(8,128)(2,1)S(1)}, bf16[2,2,256,768]{3,2,1,0:T(8,128)(2,1)}, u32[]{:S(2)}) copy-start(bf16[2,2,256,768]{3,2,1,0:T(8,128)(2,1)} %copy-done.5) | copy-start | bytes 4718596
  295.6 8.9 %slice-start.1 = ((s8[4718592]{0:T(1024)(128)(4,1)}), s8[524288]{0:T(1024)(128)(4,1)S(1)}, s32[]{:S(2)}) async-start(s8[4718592]{0:T(1024)(128)(4,1)} %bitcast.225), calls=%async_computation.2 | async-start | bytes 1048576
  300.2 29.5 %collective-permute-start.21 = (bf16[768,3,192]{0,2,1:T(8,128)(2,1)S(1)}, bf16[768,3,192]{0,2,1:T(8,128)(2,1)S(1)}, u32[]{:S(2)}, u32[]{:S(2)}) collective-permute-start(bf16[768,3,192]{0,2,1:T(8,128)(2,1)S(1)} %slice.287), channel_id=1, source_target_pairs={{0,2},{1,3},{2,0},{3,1},{4,6},{5,7},{6,4},{7,5},{8,10},{9,11},{10,... | collective-permute-start | bytes 2654216 | tf_op jit(solution)/shard_map/ppermute | solution.py:155
  303.2 25.7 %collective-permute-start.23 = (bf16[192,768]{1,0:T(8,128)(2,1)S(1)}, bf16[192,768]{1,0:T(8,128)(2,1)S(1)}, u32[]{:S(2)}, u32[]{:S(2)}) collective-permute-start(bf16[192,768]{1,0:T(8,128)(2,1)S(1)} %bitcast.242), channel_id=1, source_target_pairs={{0,2},{1,3},{2,0},{3,1},{4,6},{5,7},{6,4},{7,5},{8,10},{9,11},{10,... | collective-permute-start | bytes 884744 | tf_op jit(solution)/shard_map/ppermute | solution.py:155
  336.9 28.0 %copy-start.23 = (f32[3,6,64]{2,1,0:T(8,128)S(1)}, f32[3,6,64]{2,1,0:T(8,128)}, u32[]{:S(2)}) copy-start(f32[3,6,64]{2,1,0:T(8,128)} %get-tuple-element.51) | copy-start | bytes 13828
  336.9 91.1 %collective-permute-start.20 = (f32[256,768]{1,0:T(8,128)S(1)}, f32[256,768]{1,0:T(8,128)S(1)}, u32[]{:S(2)}, u32[]{:S(2)}) collective-permute-start(f32[256,768]{1,0:T(8,128)S(1)} %get-tuple-element.68), channel_id=1, source_target_pairs={{0,2},{1,3},{2,0},{3,1},{4,6},{5,7},{6,4},{7,5},{8,10},{9,11},{10,... | collective-permute-start | bytes 2359304 | tf_op jit(solution)/shard_map/ppermute | solution.py:155
  338.7 50.6 %copy-start.28 = (f32[768]{0:T(1024)S(1)}, f32[768]{0:T(1024)}, u32[]{:S(2)}) copy-start(f32[768]{0:T(1024)} %get-tuple-element.53) | copy-start | bytes 9220
  339.5 49.8 %copy-start.29 = (f32[768]{0:T(1024)S(1)}, f32[768]{0:T(1024)}, u32[]{:S(2)}) copy-start(f32[768]{0:T(1024)} %get-tuple-element.26) | copy-start | bytes 9220
  339.5 49.8 %copy-start.30 = (f32[768]{0:T(1024)S(1)}, f32[768]{0:T(1024)}, u32[]{:S(2)}) copy-start(f32[768]{0:T(1024)} %get-tuple-element.30) | copy-start | bytes 9220
  339.5 49.8 %copy-start.31 = (f32[768]{0:T(1024)S(1)}, f32[768]{0:T(1024)}, u32[]{:S(2)}) copy-start(f32[768]{0:T(1024)} %get-tuple-element.55) | copy-start | bytes 9220
  339.5 49.8 %copy-start.32 = (f32[768]{0:T(1024)S(1)}, f32[768]{0:T(1024)}, u32[]{:S(2)}) copy-start(f32[768]{0:T(1024)} %get-tuple-element.31) | copy-start | bytes 9220
  339.5 49.8 %copy-start.33 = (f32[768]{0:T(1024)S(1)}, f32[768]{0:T(1024)}, u32[]{:S(2)}) copy-start(f32[768]{0:T(1024)} %get-tuple-element.28) | copy-start | bytes 9220
  339.5 27.0 %collective-permute-start.13 = (bf16[256,768]{1,0:T(8,128)(2,1)}, bf16[256,768]{1,0:T(8,128)(2,1)S(1)}, u32[]{:S(2)}, u32[]{:S(2)}) collective-permute-start(bf16[256,768]{1,0:T(8,128)(2,1)} %get-tuple-element.73), channel_id=1, source_target_pairs={{0,2},{1,3},{2,0},{3,1},{4,6},{5,7},{6,4},{7,5},{8,10},{9,11},{10,... | collective-permute-start | bytes 1179656 | tf_op jit(solution)/shard_map/ppermute | solution.py:155
  340.5 24.3 %collective-permute-start.25 = (f32[768]{0:T(1024)S(1)}, f32[768]{0:T(1024)S(1)}, u32[]{:S(2)}, u32[]{:S(2)}) collective-permute-start(f32[768]{0:T(1024)S(1)} %slice.206), channel_id=1, source_target_pairs={{0,2},{1,3},{2,0},{3,1},{4,6},{5,7},{6,4},{7,5},{8,10},{9,11},{10,... | collective-permute-start | bytes 9224 | tf_op jit(solution)/shard_map/ppermute | solution.py:155
  365.0 3.6 collective-permute-start.22
  470.7 4.4 copy-start.11
  (22 other events, 52.0 us)
Sparse Core Ops, SparseCore 0:
  331.0 139.7 all-reduce.5

commit v2 on v1

v2 whole, which is shorter than its diff:
```python
import functools

import jax
import jax.numpy as jnp
from jax import lax
from jax.experimental import pallas as pl
from jax.experimental.pallas import tpu as pltpu
from jax.sharding import PartitionSpec as P

HD = 64
EPSILON = 1e-05
SCALE = HD ** (-0.5)
EXP2_SCALE = SCALE * 1.4426950408889634
GELU_A = 0.7978845608028654
GELU_B = 0.044715
T = 256
F32 = jnp.float32
BF16 = jnp.bfloat16
NN = (((1,), (0,)), ((), ()))
NT = (((1,), (1,)), ((), ()))
TN = (((0,), (0,)), ((), ()))
MESH = pl.DeviceIdType.MESH
GROUP = 8


def dot(a, b, dims=NN):
    return lax.dot_general(a, b, dims, preferred_element_type=F32)


def sub_rows(base, size, chunk, body):
    def step(i, carry):
        body(pl.ds(pl.multiple_of(base + i * chunk, chunk), chunk), i * chunk)
        return carry

    lax.fori_loop(0, size // chunk, step, 0)


class Links:
    def __init__(self, send_sems, recv_sems):
        self.send_sems, self.recv_sems = send_sems, recv_sems
        self.copies = []
        self.sent = []

    def send(self, source, target, device):
        index = len(self.copies)
        copy = pltpu.make_async_remote_copy(
            src_ref=source,
            dst_ref=target,
            send_sem=self.send_sems.at[index],
            recv_sem=self.recv_sems.at[index],
            device_id=device,
            device_id_type=MESH,
        )
        copy.start()
        self.copies.append(copy)
        return copy

    def wait_send(self, copy):
        copy.wait_send()
        self.sent.append(copy)

    def finish(self):
        for copy in self.copies:
            if not any(copy is other for other in self.sent):
                copy.wait_send()


def layer_kernel(
    dp_size,
    tok_ref,
    cot_ref,
    info_ref,
    vec_ref,
    bias_ref,
    wqkv_ref,
    wout_ref,
    wfc_ref,
    wproj_ref,
    out_ref,
    tgrad_ref,
    dproj_ref,
    dfc_ref,
    dattn_ref,
    small_ref,
    tok_in,
    cot_in,
    info_buf,
    bias_in,
    wqkv_in,
    wout_all,
    wfc_in,
    wproj_in,
    count_out,
    count_in,
    seg_col,
    weight_col,
    normed,
    normed2,
    grad_full,
    attn_grad,
    q_s,
    k_s,
    v_s,
    o_s,
    do_s,
    p0,
    p1,
    p2,
    p3,
    att,
    middle,
    hid,
    dpre,
    give,
    got,
    own,
    give2,
    got2,
    key_acc,
    value_acc,
    acc_half,
    acc_attn,
    x_give,
    x_got,
    y_got,
    z_got,
    out_give,
    tg_give,
    tg_got,
    small_a,
    small_in,
    small_b,
    small_dp,
    send_sems,
    recv_sems,
    local_sems,
):
    d = lax.axis_index("dp")
    t = lax.axis_index("tp")
    x = t // 2
    c = t - 2 * x
    t_core = t + 1 - 2 * c
    t_chip = lax.rem(t + 2, 4)
    t_both = 3 - t
    y = lax.rem(d, 2)
    group_first = d - lax.rem(d, GROUP)
    place = d - group_first
    z = place // 2
    d_y = d + 1 - 2 * y

    def d_flip(bit):
        size = 1 << bit
        return d + size - 2 * size * lax.rem(d // size, 2)

    def d_z(step):
        return group_first + 2 * lax.rem(z + step, 4) + y

    dqkv = hid
    count_bits = dp_size.bit_length() - 1
    links = Links(send_sems, recv_sems)
    send = links.send

    barrier = pltpu.get_barrier_semaphore()
    peers = [(d, t_core), (d, t_chip), (d, t_both)]
    peers += [(group_first + lax.rem(place + k, GROUP), t) for k in range(1, GROUP)]
    peers += [(d_flip(bit), t) for bit in range(3, count_bits)]
    for peer in peers:
        pl.semaphore_signal(barrier, inc=1, device_id=peer, device_id_type=MESH)
    pl.semaphore_wait(barrier, len(peers))

    def block_rows(index):
        return pl.ds(pl.multiple_of(index * T, T), T)

    gain1, shift1, out_bias = vec_ref[0:1, :], vec_ref[1:2, :], vec_ref[2:3, :]
    gain2, shift2, proj_bias = vec_ref[3:4, :], vec_ref[4:5, :], vec_ref[5:6, :]

    tok_copy = send(tok_ref.at[1 - x], tok_in, (d, t_chip))
    info_buf[t] = info_ref[x]
    info_copies = [
        send(info_ref.at[x], info_buf.at[t], (d, t_core)),
        send(info_ref.at[1 - x], info_buf.at[t], (d, t_chip)),
        send(info_ref.at[1 - x], info_buf.at[t], (d, t_both)),
    ]
    bias_copy = send(bias_ref, bias_in, (d, t_chip))
    wout_all[0:192, :] = wout_ref[...]
    for ref in (small_a, count_out):
        ref[...] = jnp.zeros_like(ref)

    def moments(values):
        average = jnp.mean(values, axis=-1, keepdims=True)
        centered = values - average
        spread = jnp.mean(centered * centered, axis=-1, keepdims=True)
        inverse = lax.rsqrt(spread + EPSILON)
        return centered * inverse, inverse

    def norm_one(load, index):
        base = index * T

        def body(rows, at):
            scaled, _ = moments(load(at))
            normed[rows, :] = (scaled * gain1 + shift1).astype(BF16)

        sub_rows(base, T, 64, body)

    def tok_own(at):
        return tok_ref[x, pl.ds(at, 64), :].astype(F32)

    def tok_other(at):
        return tok_in[pl.ds(at, 64), :].astype(F32)

    norm_one(tok_own, t)
    normed_copies = [send(normed.at[block_rows(t)], normed.at[block_rows(t)], (d, t_core))]
    tok_copy.wait_recv()
    wqkv_half = pl.ds(pl.multiple_of(y * 288, 16), 288)
    wout_half = pl.ds(pl.multiple_of(y * 96, 16), 96)
    wout_half_in = pl.ds(pl.multiple_of(192 + y * 96, 16), 96)
    w_half = pl.ds(pl.multiple_of(y * 384, 16), 384)
    wqkv_x = send(wqkv_ref.at[wqkv_half], wqkv_in.at[wqkv_half], (d, t_chip))
    wout_x = send(wout_ref.at[wout_half], wout_all.at[wout_half_in], (d, t_chip))
    norm_one(tok_other, t_chip)
    normed_copies.append(
        send(normed.at[block_rows(t_chip)], normed.at[block_rows(t_chip)], (d, t_core))
    )
    for copy in info_copies:
        copy.wait_recv()

    half = info_buf[0, 2:3, 0:1]
    count = jnp.sum(info_buf[0, 1:2, :], axis=1, keepdims=True)
    for index in range(1, 4):
        count = count + jnp.sum(info_buf[index, 1:2, :], axis=1, keepdims=True)
    counts = [count * (1.0 - half), count * half]
    count_peers = [(d, t_chip)] + [(d_flip(bit), t) for bit in range(count_bits)]
    count_copies = []

    def count_start():
        step = len(count_copies)
        if step < len(count_peers):
            count_out[step, 0:1, :] = jnp.broadcast_to(counts[0], (1, 128))
            count_out[step, 1:2, :] = jnp.broadcast_to(counts[1], (1, 128))
            count_copies.append(send(count_out.at[step], count_in.at[step], count_peers[step]))

    def count_end():
        step = len(count_copies) - 1
        count_copies[step].wait_recv()
        counts[0] = counts[0] + count_in[step, 0:1, 0:1]
        counts[1] = counts[1] + count_in[step, 1:2, 0:1]

    count_start()
    seg_row = jnp.concatenate([info_buf[i, 0:1, :] for i in range(4)], axis=1)
    for index in range(4):
        row = jnp.broadcast_to(info_buf[index, 0:1, :], (128, T))
        seg_col[index * T : (index + 1) * T, :] = row.T
    for copy in normed_copies:
        copy.wait_recv()

    def project(side, weight):
        bias = (bias_ref if side == 0 else bias_in)[1:2, 0:576]

        def body(rows, at):
            value = (dot(normed[rows, :], weight[...], NT) + bias).astype(BF16)
            for part, ref in enumerate((q_s, k_s, v_s)):
                for h in range(3):
                    lane = part * 192 + h * HD
                    ref[3 * side + h, rows, :] = value[:, lane : lane + HD]

        sub_rows(0, 4 * T, T, body)

    p_refs = (p0, p1, p2, p3)

    def attend(side):
        def head(h, carry):
            for index, p_ref in enumerate(p_refs):
                start, stop = index * T, (index + 1) * T
                rows = slice(start, stop)
                scores = dot(q_s[h, rows, :], k_s[h, 0:stop, :], NT) * EXP2_SCALE
                query_at = start + lax.broadcasted_iota(jnp.int32, (T, stop), 0)
                key_at = lax.broadcasted_iota(jnp.int32, (T, stop), 1)
                allowed = (key_at <= query_at) & (seg_col[rows, 0:1] == seg_row[:, 0:stop])
                scores = jnp.where(allowed, scores, -1e30)
                top = jnp.max(scores, axis=1, keepdims=True)
                exponent = jnp.exp2(scores - top)
                inverse = 1.0 / jnp.sum(exponent, axis=1, keepdims=True)
                low = (exponent * inverse).astype(BF16)
                p_ref[h] = low
                o_s[h, rows, :] = dot(low, v_s[h, 0:stop, :]).astype(BF16)
            return carry

        lax.fori_loop(3 * side, 3 * side + 3, head, 0)

    project(0, wqkv_ref)
    attend(0)
    count_end()
    count_start()
    wqkv_x.wait_recv()
    wqkv_y = send(wqkv_in.at[wqkv_half], wqkv_in.at[wqkv_half], (d_y, t))
    wout_x.wait_recv()
    wout_y = send(wout_all.at[wout_half_in], wout_all.at[wout_half_in], (d_y, t))
    cot_copy = send(cot_ref.at[1 - x], cot_in, (d, t_chip))
    wfc_x = send(wfc_ref.at[w_half], wfc_in.at[w_half], (d, t_chip))
    bias_copy.wait_recv()
    wqkv_y.wait_recv()
    project(1, wqkv_in)
    wproj_x = send(wproj_ref.at[w_half], wproj_in.at[w_half], (d, t_chip))
    attend(1)
    count_end()
    count_start()
    for h in range(6):
        att[:, h * HD : (h + 1) * HD] = o_s[h]

    def scatter(partial, give_ref, got_ref, before=()):
        for copy in before:
            links.wait_send(copy)
        copies = []
        for slot, index in enumerate((t_core, t_both)):
            give_ref[slot] = partial(index).astype(BF16)
            copies.append(send(give_ref.at[slot], got_ref.at[slot], (d, t_core)))
        for slot, index in enumerate((t, t_chip)):
            own[slot] = partial(index)
        return copies

    def out_partial(index):
        return dot(att[block_rows(index), :], wout_all[...])

    wout_y.wait_recv()
    attn_copies = scatter(out_partial, give, got)
    wfc_x.wait_recv()
    wfc_y = send(wfc_in.at[w_half], wfc_in.at[w_half], (d_y, t))
    count_end()
    count_start()

    normed2_copies = []
    for slot, index in enumerate((t, t_chip)):
        attn_copies[slot].wait_recv()
        load = tok_own if slot == 0 else tok_other

        def body(rows, at, slot=slot, index=index, load=load):
            value = load(at) + own[slot, rows, :] + got[slot, rows, :].astype(F32) + out_bias
            middle[slot, rows, :] = value
            scaled, _ = moments(value)
            normed2[pl.ds(pl.multiple_of(index * T + at, 64), 64), :] = (
                scaled * gain2 + shift2
            ).astype(BF16)

        sub_rows(0, T, 64, body)
        rows = block_rows(index)
        normed2_copies.append(send(normed2.at[rows], normed2.at[rows], (d, t_core)))
    while len(count_copies) < len(count_peers):
        count_end()
        count_start()
    count_end()

    row_scale = (counts[0] + counts[1]) / (2.0 * jnp.where(half == 0.0, counts[0], counts[1]))
    cot_copy.wait_recv()
    grad_copies = []
    for slot, index in enumerate((t, t_chip)):
        row = jnp.broadcast_to(info_buf[index, 1:2, :] * row_scale, (128, T))
        weight_col[slot] = row.T

    def out_grad(slot, rows, at):
        source = cot_ref[x, rows, :] if slot == 0 else cot_in[rows, :]
        return source.astype(F32) * weight_col[slot, rows, 0:1]

    for slot, index in enumerate((t, t_chip)):

        def body(rows, at, slot=slot, index=index):
            low = out_grad(slot, rows, at).astype(BF16)
            grad_full[pl.ds(pl.multiple_of(index * T + at, 64), 64), :] = low
            small_a[0, 5:6, :] += jnp.sum(low.astype(F32), axis=0, keepdims=True)

        sub_rows(0, T, 64, body)
        rows = block_rows(index)
        grad_copies.append(send(grad_full.at[rows], grad_full.at[rows], (d, t_core)))
    for copy in normed2_copies + grad_copies:
        copy.wait_recv()

    def mlp(side, fc, proj):
        bias = (bias_ref if side == 0 else bias_in)[0:1, :]

        def body(rows, at):
            pre = dot(normed2[rows, :], fc[...]) + bias
            square = pre * pre
            bent = jnp.tanh(GELU_A * (pre + GELU_B * square * pre))
            rise = 0.5 * (1.0 + bent)
            hid[side, rows, :] = (pre * rise).astype(BF16)
            slope = rise + 0.5 * pre * (1.0 - bent * bent) * (
                GELU_A + (3.0 * GELU_A * GELU_B) * square
            )
            low = (dot(grad_full[rows, :], proj[...], NT) * slope).astype(BF16)
            dpre[side, rows, :] = low
            small_a[0, 6 + 2 * side : 7 + 2 * side, :] += jnp.sum(
                low.astype(F32), axis=0, keepdims=True
            )

        sub_rows(0, 4 * T, T, body)

    mlp(0, wfc_ref, wproj_ref)
    wproj_x.wait_recv()
    wproj_y = send(wproj_in.at[w_half], wproj_in.at[w_half], (d_y, t))
    wfc_y.wait_recv()
    wproj_y.wait_recv()
    mlp(1, wfc_in, wproj_in)

    def weight_rows(body):
        sub_rows(0, 768, T, lambda rows, at: body(rows))

    def x_start(m, product):
        def body(rows):
            x_give[m, rows, :] = product(rows).astype(BF16)

        weight_rows(body)
        return send(x_give.at[m], x_got.at[m], (d, t_chip))

    def half_rows(index):
        return pl.ds(pl.multiple_of(index * 384, 384), 384)

    def y_start(m, product):
        other, mine = half_rows(1 - y), half_rows(y)
        x_got[m, other, :] = (product(other) + x_got[m, other, :].astype(F32)).astype(BF16)
        copy = send(x_got.at[m, other], y_got.at[m], (d_y, t))
        acc_half[m] = product(mine) + x_got[m, mine, :].astype(F32)
        return copy

    def quarter(index):
        return pl.ds(pl.multiple_of(index * 96, 96), 96)

    def quarter_sum(m, index):
        local = quarter(index)
        if m == 2:
            mine = acc_attn[pl.ds(pl.multiple_of(y * 384 + index * 96, 96), 96), :]
        else:
            mine = acc_half[m, local, :]
        return mine + y_got[m, local, :].astype(F32)

    def z_start(m):
        copies = []
        for step in range(1, 4):
            rows = quarter(lax.rem(z + step, 4))
            y_got[m, rows, :] = quarter_sum(m, lax.rem(z + step, 4)).astype(BF16)
            copies.append(send(y_got.at[m, rows], z_got.at[m, step - 1], (d_z(step), t)))
        return copies

    weight_outs = (dproj_ref, dfc_ref, dattn_ref)

    def z_end(m):
        total = quarter_sum(m, z)
        for step in range(3):
            total = total + z_got[m, step].astype(F32)
        y_got[m, quarter(z), :] = total.astype(BF16)
        fin = y_got.at[m, quarter(z)]
        rows = pl.ds(pl.multiple_of(y * 384 + z * 96, 96), 96)
        keep = pltpu.make_async_copy(fin, weight_outs[m].at[rows], local_sems.at[m])
        keep.start()
        spread = [send(fin, weight_outs[m].at[rows], (d_z(step), t)) for step in range(1, 4)]
        across = [send(fin, weight_outs[m].at[rows], (d_y, t))]
        return keep, spread, across

    def spread_on(m, state):
        _, spread, across = state
        for step in range(1, 4):
            spread[step - 1].wait_recv()
            source = lax.rem(z + 4 - step, 4)
            rows = pl.ds(pl.multiple_of(y * 384 + source * 96, 96), 96)
            across.append(send(weight_outs[m].at[rows], weight_outs[m].at[rows], (d_y, t)))

    def spread_end(state):
        keep, _, across = state
        keep.wait()
        for copy in across:
            copy.wait_recv()

    def proj_product(side):
        return lambda rows: dot(hid[side, :, rows], grad_full[...], TN)

    def fc_product(side):
        return lambda rows: dot(normed2[:, rows], dpre[side], TN)

    proj_x = x_start(0, proj_product(1))
    fc_x = x_start(1, fc_product(1))

    def mlp_partial(index):
        rows = block_rows(index)
        return dot(hid[0, rows, :], wproj_ref[...]) + dot(hid[1, rows, :], wproj_in[...])

    mlp_copies = scatter(mlp_partial, give2, got2)
    for slot in range(2):
        mlp_copies[slot].wait_recv()

        def body(rows, at, slot=slot):
            value = (
                middle[slot, rows, :]
                + own[slot, rows, :]
                + got2[slot, rows, :].astype(F32)
                + proj_bias
            )
            if slot == 0:
                out_ref[x, rows, :] = value.astype(BF16)
            else:
                out_give[rows, :] = value.astype(BF16)

        sub_rows(0, T, 64, body)
    out_copy = send(out_give, out_ref.at[x], (d, t_chip))

    def norm2_partial(index):
        rows = block_rows(index)
        return dot(dpre[0, rows, :], wfc_ref[...], NT) + dot(dpre[1, rows, :], wfc_in[...], NT)

    back_copies = scatter(norm2_partial, give, got, attn_copies)
    def norm_back(upstream, values, gain):
        scaled, inverse = moments(values)
        pushed = upstream * gain
        mean_one = jnp.mean(pushed, axis=-1, keepdims=True)
        mean_two = jnp.mean(pushed * scaled, axis=-1, keepdims=True)
        gain_grad = jnp.sum(upstream * scaled, axis=0, keepdims=True)
        shift_grad = jnp.sum(upstream, axis=0, keepdims=True)
        return inverse * (pushed - mean_one - scaled * mean_two), gain_grad, shift_grad

    grad_copies = []
    for slot, index in enumerate((t, t_chip)):
        back_copies[slot].wait_recv()

        def body(rows, at, slot=slot, index=index):
            upstream = own[slot, rows, :] + got[slot, rows, :].astype(F32)
            part, gain_grad, shift_grad = norm_back(upstream, middle[slot, rows, :], gain2)
            value = out_grad(slot, rows, at) + part
            middle[slot, rows, :] = value
            low = value.astype(BF16)
            attn_grad[pl.ds(pl.multiple_of(index * T + at, 64), 64), :] = low
            small_a[0, 2:3, :] += gain_grad
            small_a[0, 3:4, :] += shift_grad
            small_a[0, 4:5, :] += jnp.sum(low.astype(F32), axis=0, keepdims=True)

        sub_rows(0, T, 64, body)
        rows = block_rows(index)
        grad_copies.append(send(attn_grad.at[rows], attn_grad.at[rows], (d, t_core)))
    for copy in grad_copies:
        copy.wait_recv()

    def spread_heads(rows, at):
        value = dot(attn_grad[rows, :], wout_all[...], NT)
        for h in range(6):
            do_s[h, rows, :] = value[:, h * HD : (h + 1) * HD].astype(BF16)

    sub_rows(0, 4 * T, T, spread_heads)
    x_give[2, 576:768, :] = dot(att[:, 192:384], attn_grad[...], TN).astype(BF16)
    out_x = send(x_give.at[2, 576:768], x_got.at[2, 576:768], (d, t_chip))
    acc_attn[576:768, :] = dot(att[:, 0:192], attn_grad[...], TN)
    proj_x.wait_recv()
    proj_y = y_start(0, proj_product(0))

    def attend_back(side):
        def head(h, carry):
            query_t = q_s[h].T
            for index, p_ref in enumerate(p_refs):
                start, stop = index * T, (index + 1) * T
                rows = slice(start, stop)
                weights = p_ref[h]
                upstream = do_s[h, rows, :]
                row_dot = jnp.sum(
                    upstream.astype(F32) * o_s[h, rows, :].astype(F32), axis=1, keepdims=True
                )
                weight_grad = dot(upstream, v_s[h, 0:stop, :], NT)
                score_grad = (weights.astype(F32) * (weight_grad - row_dot)).astype(BF16)
                q_s[h, rows, :] = (dot(score_grad, k_s[h, 0:stop, :]) * SCALE).astype(BF16)
                key_part = dot(query_t[:, rows], score_grad)
                value_part = dot(upstream.T, weights)
                if start:
                    key_acc[:, 0:start] += key_part[:, 0:start]
                    value_acc[:, 0:start] += value_part[:, 0:start]
                key_acc[:, rows] = key_part[:, start:]
                value_acc[:, rows] = value_part[:, start:]
            k_s[h] = (key_acc[...] * SCALE).T.astype(BF16)
            v_s[h] = value_acc[...].T.astype(BF16)
            return carry

        lax.fori_loop(3 * side, 3 * side + 3, head, 0)
        for part, ref in enumerate((q_s, k_s, v_s)):
            for h in range(3):
                lane = part * 192 + h * HD
                dqkv[side, :, lane : lane + HD] = ref[3 * side + h]
        small_a[0, 7 + 2 * side : 8 + 2 * side, 0:576] = jnp.sum(
            dqkv[side, :, 0:576].astype(F32), axis=0, keepdims=True
        )

    attend_back(1)
    for start in range(0, 576, 192):
        x_give[2, start : start + 192, :] = dot(
            dqkv[1, :, start : start + 192], normed[...], TN
        ).astype(BF16)
    qkv_x = send(x_give.at[2, 0:576], x_got.at[2, 0:576], (d, t_chip))

    proj_y.wait_recv()
    proj_z = z_start(0)
    fc_x.wait_recv()
    fc_y = y_start(1, fc_product(0))
    attend_back(0)

    def norm1_partial(index):
        rows = block_rows(index)
        return dot(dqkv[0, rows, 0:576], wqkv_ref[...]) + dot(dqkv[1, rows, 0:576], wqkv_in[...])

    back_copies = scatter(norm1_partial, give, got, back_copies)
    for copy in proj_z:
        copy.wait_recv()
    proj_state = z_end(0)
    fc_y.wait_recv()
    fc_z = z_start(1)
    for slot in (1, 0):
        back_copies[slot].wait_recv()
        load = tok_own if slot == 0 else tok_other

        def body(rows, at, slot=slot, load=load):
            upstream = own[slot, rows, :] + got[slot, rows, :].astype(F32)
            part, gain_grad, shift_grad = norm_back(upstream, load(at), gain1)
            value = middle[slot, rows, :] + part
            if slot == 0:
                own[0, rows, :] = value
            else:
                tg_give[rows, :] = value.astype(BF16)
            small_a[0, 0:1, :] += gain_grad
            small_a[0, 1:2, :] += shift_grad

        sub_rows(0, T, 64, body)
        if slot == 1:
            tg_copy = send(tg_give, tg_got, (d, t_chip))
    tg_keep = [pltpu.make_async_copy(own.at[0], tgrad_ref.at[x], local_sems.at[3])]
    tg_keep[0].start()

    small_copies = [
        send(small_a.at[0], small_in.at[0], (d, t_core)),
        send(small_a.at[0], small_in.at[1], (d, t_chip)),
        send(small_a.at[0], small_in.at[2], (d, t_both)),
    ]
    for start in range(0, 576, 192):
        acc_attn[start : start + 192, :] = dot(
            dqkv[0, :, start : start + 192], normed[...], TN
        )
    out_x.wait_recv()
    qkv_x.wait_recv()

    def add_received(rows):
        acc_attn[rows, :] += x_got[2, rows, :].astype(F32)

    weight_rows(add_received)
    x_got[2, half_rows(1 - y), :] = acc_attn[half_rows(1 - y), :].astype(BF16)
    attn_y = send(x_got.at[2, half_rows(1 - y)], y_got.at[2], (d_y, t))
    for copy in fc_z:
        copy.wait_recv()
    fc_state = z_end(1)
    spread_on(0, proj_state)

    for copy in small_copies:
        copy.wait_recv()
    small_b[0:6, :] = (
        small_a[0, 0:6, :] + small_in[0, 0:6, :] + small_in[1, 0:6, :] + small_in[2, 0:6, :]
    )
    small_b[6:8, :] = small_a[0, 6:8, :] + small_in[1, 8:10, :]
    small_dp_copies = [
        send(small_b, small_dp.at[k - 1], (group_first + lax.rem(place + k, GROUP), t))
        for k in range(1, GROUP)
    ]
    attn_y.wait_recv()
    attn_z = z_start(2)
    for copy in small_dp_copies:
        copy.wait_recv()
    total = small_b[...]
    for k in range(GROUP - 1):
        total = total + small_dp[k]
    small_ref[...] = total
    tg_copy.wait_recv()
    own[1] = tg_got[...].astype(F32)
    tg_keep.append(pltpu.make_async_copy(own.at[1], tgrad_ref.at[1 - x], local_sems.at[4]))
    tg_keep[1].start()
    spread_on(1, fc_state)
    for copy in attn_z:
        copy.wait_recv()
    attn_state = z_end(2)
    spread_on(2, attn_state)
    out_copy.wait_recv()
    for state in (proj_state, fc_state, attn_state):
        spread_end(state)
    for copy in tg_keep:
        copy.wait()
    links.finish()


VMEM = pl.BlockSpec(memory_space=pltpu.VMEM)
ANY = pl.BlockSpec(memory_space=pl.ANY)


def local(
    dp_size,
    tokens,
    cotangent,
    segment_ids,
    valid_mask,
    row_half,
    norm1_gain,
    norm1_shift,
    qkv_weight,
    qkv_bias,
    out_weight,
    out_bias,
    norm2_gain,
    norm2_shift,
    fc_weight,
    fc_bias,
    proj_weight,
    proj_bias,
):
    half_rows = jnp.broadcast_to(row_half[:, None], segment_ids.shape)
    empty = jnp.zeros_like(segment_ids)
    info = jnp.stack([segment_ids, valid_mask, half_rows] + [empty] * 5, axis=1).astype(F32)
    nothing = jnp.zeros_like(out_bias)
    vectors = jnp.stack(
        [norm1_gain, norm1_shift, out_bias, norm2_gain, norm2_shift, proj_bias, nothing, nothing]
    )
    flat_bias = jnp.concatenate([qkv_bias.reshape(576), jnp.zeros((192,), F32)])
    biases = jnp.stack([fc_bias, flat_bias] + [nothing] * 6)
    qkv_rows = jnp.transpose(qkv_weight, (1, 2, 0)).reshape(576, 768)

    copies = 128

    def buffer(shape, dtype):
        return pltpu.VMEM(shape, dtype)

    outs = pl.pallas_call(
        functools.partial(layer_kernel, dp_size),
        out_shape=(
            jax.ShapeDtypeStruct((2, T, 768), BF16),
            jax.ShapeDtypeStruct((2, T, 768), F32),
            jax.ShapeDtypeStruct((768, 768), BF16),
            jax.ShapeDtypeStruct((768, 768), BF16),
            jax.ShapeDtypeStruct((768, 768), BF16),
            jax.ShapeDtypeStruct((8, 768), F32),
        ),
        in_specs=[VMEM] * 9,
        out_specs=(VMEM, ANY, ANY, ANY, ANY, VMEM),
        scratch_shapes=[
            buffer((T, 768), BF16),
            buffer((T, 768), BF16),
            buffer((4, 8, T), F32),
            buffer((8, 768), F32),
            buffer((576, 768), BF16),
            buffer((384, 768), BF16),
            buffer((768, 768), BF16),
            buffer((768, 768), BF16),
            buffer((8, 8, 128), F32),
            buffer((8, 8, 128), F32),
            buffer((1024, 128), F32),
            buffer((2, T, 128), F32),
            buffer((1024, 768), BF16),
            buffer((1024, 768), BF16),
            buffer((1024, 768), BF16),
            buffer((1024, 768), BF16),
            buffer((6, 1024, HD), BF16),
            buffer((6, 1024, HD), BF16),
            buffer((6, 1024, HD), BF16),
            buffer((6, 1024, HD), BF16),
            buffer((6, 1024, HD), BF16),
            buffer((6, T, T), BF16),
            buffer((6, T, 2 * T), BF16),
            buffer((6, T, 3 * T), BF16),
            buffer((6, T, 4 * T), BF16),
            buffer((1024, 384), BF16),
            buffer((2, T, 768), F32),
            buffer((2, 1024, 768), BF16),
            buffer((2, 1024, 768), BF16),
            buffer((2, T, 768), BF16),
            buffer((2, T, 768), BF16),
            buffer((2, T, 768), F32),
            buffer((2, T, 768), BF16),
            buffer((2, T, 768), BF16),
            buffer((HD, 1024), F32),
            buffer((HD, 1024), F32),
            buffer((2, 384, 768), F32),
            buffer((768, 768), F32),
            buffer((3, 768, 768), BF16),
            buffer((3, 768, 768), BF16),
            buffer((3, 384, 768), BF16),
            buffer((3, 3, 96, 768), BF16),
            buffer((T, 768), BF16),
            buffer((T, 768), BF16),
            buffer((T, 768), BF16),
            buffer((1, 16, 768), F32),
            buffer((3, 16, 768), F32),
            buffer((8, 768), F32),
            buffer((7, 8, 768), F32),
            pltpu.SemaphoreType.DMA((copies,)),
            pltpu.SemaphoreType.DMA((copies,)),
            pltpu.SemaphoreType.DMA((5,)),
        ],
        compiler_params=pltpu.CompilerParams(
            collective_id=0, has_side_effects=True, vmem_limit_bytes=66500000
        ),
    )(
        tokens,
        cotangent,
        info,
        vectors,
        biases,
        qkv_rows,
        out_weight,
        fc_weight,
        proj_weight,
    )
    output, tokens_grad, dproj, dfc, dattn, small = outs

    def all_groups(value):
        if dp_size == GROUP:
            return value.astype(F32)
        sets = [[g * GROUP + i for g in range(dp_size // GROUP)] for i in range(GROUP)]
        return lax.psum(value.astype(F32), "dp", axis_index_groups=sets)

    dproj, dfc, dattn, small = map(all_groups, (dproj, dfc, dattn, small))
    dqkv_weight = jnp.transpose(dattn[:576].reshape(3, 192, 768), (2, 0, 1))
    return (
        output,
        tokens_grad,
        small[0],
        small[1],
        dqkv_weight,
        small[7, :576].reshape(3, 192),
        dattn[576:],
        small[4],
        small[2],
        small[3],
        dfc,
        small[6],
        dproj,
        small[5],
    )


def solution(mesh):
    row, flat = P("dp", "tp", None), P("dp", "tp")
    in_specs = (
        row,
        row,
        flat,
        flat,
        P("dp"),
        P(),
        P(),
        P(None, None, "tp"),
        P(None, "tp"),
        P("tp", None),
        P(),
        P(),
        P(),
        P(None, "tp"),
        P("tp"),
        P("tp", None),
        P(),
    )
    out_specs = (
        row,
        row,
        P(),
        P(),
        P(None, None, "tp"),
        P(None, "tp"),
        P("tp", None),
        P(),
        P(),
        P(),
        P(None, "tp"),
        P("tp"),
        P("tp", None),
        P(),
    )
    return jax.shard_map(
        functools.partial(local, mesh.shape["dp"]),
        mesh=mesh,
        in_specs=in_specs,
        out_specs=out_specs,
        check_vma=False,
    )
```

time: 493 us -> 253 us (0.51)
  Pallas kernels: 39.7 us -> 226 us
  blocking collectives: 153 us -> 0 us
  waiting for transfers between devices: 128 us -> 0 us
  other arithmetic: 48.2 us -> 4.44 us
  matrix products: 40.3 us -> 0 us
  starting transfers between devices: 26.4 us -> 0 us
  between operations: 17.8 us -> 0.69 us
  local copies, waits for them, and re-layouts: 32.3 us -> 18.2 us
    pallas_call x2 -> x1, Pallas kernels: 39.7 us -> 226 us  [local(): pl.pallas_call(functools.partial(layer_kernel, dp_size), out_shape=(jax.S...]
    psum x3 -> x0, blocking collectives: 153 us -> none  [the longest x1 93.2 us: local(): lax.psum((replay_local, fresh_local), ('dp', 'tp'))]
    ppermute x27 -> x0, waiting for transfers between devices: 87 us -> none  [the longest x18 86.9 us: swap_chip(): return lax.ppermute(value, 'tp', [(i, i ^ 2) for i in range(4)])]
    psum x1 -> x0, waiting for transfers between devices: 41.5 us -> none  [reduce_weight(): return lax.psum(total.astype(BF16), 'dp').astype(F32)]
    dot_general x12 -> x0, matrix products: 40.3 us -> none  [the longest x4 17.5 us: dot(): return lax.dot_general(a, b, dims, preferred_element_type=F32)]
    ppermute x27 -> x0, starting transfers between devices: 26.4 us -> none  [the longest x18 24.6 us: swap_chip(): return lax.ppermute(value, 'tp', [(i, i ^ 2) for i in range(4)])]
    reduce_sum x13 -> x0, other arithmetic: 18.3 us -> none  [the longest x3 6.27 us: layer_norm(): return centered * lax.rsqrt(spread + EPSILON) * gain + shift]
    unnamed x88 -> x12, local copies, waits for them, and re-layouts: 14.8 us -> 3.39 us
  transfers between devices with their start and end apart: 28 -> 0, of which waited for: 9 -> 0; matrix products, arithmetic and copies ran while one was open for 16% -> 0% of each run, Pallas kernels for 4% -> 0%
where the time goes in v2:
time: 253 us; the launch traced here: 249 us
  Pallas kernels  226 us (89%)
  local copies, waits for them, and re-layouts  18.2 us (7%)
  other arithmetic  4.44 us (2%)
    pallas_call x1, Pallas kernels, local(): pl.pallas_call(functools.partial(layer_kernel, dp_size), out_shape=(jax.S...  226 us

profile of v2, /device:TPU:0, one launch (start us, length us, event | category | flops | bytes accessed | tf_op | source)
XLA Modules:
  0.0 249.0 jit_solution(5727163044382925237)
XLA Ops:
  0.7 0.1 pad.4.clone
  0.7 0.7 stack.45
  1.4 0.7 stack.46
  2.1 0.7 stack_broadcast_in_dim.8
  2.8 0.7 stack.49
  3.5 0.7 stack.50
  4.2 0.7 stack.51
  4.9 0.7 stack.52
  5.6 0.7 stack.53
  6.3 0.7 stack.56
  7.0 0.7 stack.54
  7.7 0.8 reshape.37
  8.4 0.6 stack.55.vec_ref
  9.1 0.6 convert_element_type.12.info_ref
  9.7 0.7 maximum_maximum_fusion.bias_ref
  10.4 225.7 %shard_map.272 = (bf16[2,256,768]{2,1,0:T(8,128)(2,1)}, f32[2,256,768]{2,1,0:T(8,128)}, bf16[768,768]{1,0:T(8,128)(2,1)}, bf16[768,768]{1,0:T(8,128)(2,1)}, bf16[768,768]{1,0:T(8,128)(2,1)}, /*index=5*/f32[8,768]{1,0:T(8,128)}) custom-call(bf16[2,256,768]{2,1,0:T(8,128)(2,1)} %tok_ref.1, bf16[2,256,768]{2,1,0:T(8,128)(2,1)} %cot_ref.1, ...), custom_call_target="tpu_custom_call" | custom-call | tf_op jit(solution)/shard_map/pallas_call | solution.py:726
  236.1 0.0 copy-start
  236.1 0.8 slice_reduce_fusion.7
  236.9 0.7 reshape_squeeze.3
  237.6 1.7 slice_reduce_fusion
  239.3 1.8 slice.41
  241.1 0.0 copy-done
  241.1 0.0 copy-start.3
  241.1 1.3 slice.40
  242.4 0.5 copy-done.3
  242.9 0.0 copy-start.2
  242.9 1.6 convert_element_type.14
  244.5 0.1 copy-done.2
  244.6 0.0 copy-start.4
  244.6 1.6 convert_element_type.15
  246.1 0.0 copy-done.4
  246.2 0.0 copy-start.1
  246.2 0.9 copy.33
  247.0 0.8 copy-done.1
  247.8 1.1 copy.34
  (7 shorter events, 0.1 us)
Async XLA Ops:
  236.1 5.0 %copy-start = (bf16[768,768]{1,0:T(8,128)(2,1)S(1)}, bf16[768,768]{1,0:T(8,128)(2,1)}, u32[]{:S(2)}) copy-start(bf16[768,768]{1,0:T(8,128)(2,1)} %get-tuple-element.23) | copy-start | bytes 3538948
  241.1 1.8 copy-start.3
  242.9 1.7 copy-start.2
  244.6 1.6 copy-start.4
  246.2 1.7 copy-start.1
